TPU v7x, 512 devices: a whole 4x8x8 slice. The times are simulated.
512 devices in a mesh: blk: 32 (over y, x), col: 16 (over z, core).
Axes of the slice: x: 4, y: 8, z: 8, core: 2. Of those that a mesh axis runs over, the one named last changes fastest.
Arguments:
- pair_occ: int32 [32, 256], P('blk', 'col'), may hold values from 0 to 3
- pair_offset: int32 [32, 256], P('blk', 'col'), may hold values from 0 to 2, as said below
- pair_other: int32 [32, 256], P('blk', 'col'), may hold values from 0 to 3
- pno_blocks: int32 [32, 256], P('blk', 'col'), may hold values from 1 to 4
- pno_coef: float32 [128, 128, 1024], P('blk'), may hold values from -0.5 to 0.5
- amplitudes: float32 [32, 256, 128, 128], P('blk', 'col'), may hold values from -0.4 to 0.4
- integrals: float32 [32, 256, 128, 128], P('blk', 'col'), may hold values from -0.5 to 0.5
Outputs:
- density: float32 [32, 1024, 1024], P('blk', None, 'col')
Inputs may be any that keep to these rules, and one draw needn't show every extreme that they name: `pair_offset`: in every device's 16 slots the first three name the offsets 0, 1 and 2 in order.
All inputs are finite; a program needn't handle non-finite values.
Results may differ from a plain program's by a relative error of at most 0.0003.
Values sent between devices are 32-bit elements; how exact they have to be, the bound alone decides.
No kernel may reach another device: no remote copies, remote signals or barrier semaphores. Data moves between devices by JAX's collectives and lax.ppermute only.
A program may use at most 64 MiB of HBM per device.

v0:
```python
import jax
import jax.numpy as jnp
from jax import lax
from jax.sharding import PartitionSpec as P


def padded(cells, sides, width):
    for axis, dim in sides:
        count = lax.axis_size(axis)
        head = lax.slice_in_dim(cells, 0, width, axis=dim)
        tail = lax.slice_in_dim(cells, cells.shape[dim] - width, cells.shape[dim], axis=dim)
        cells = jnp.concatenate(
            [
                lax.ppermute(tail, axis, [(i, (i + 1) % count) for i in range(count)]),
                cells,
                lax.ppermute(head, axis, [((i + 1) % count, i) for i in range(count)]),
            ],
            axis=dim,
        )
    return cells


def local(pair_occ, pair_offset, pair_other, pno_blocks, pno_coef, amplitudes, integrals):
    orbitals = pno_coef.shape[0]
    pno_count = pno_coef.shape[1]
    basis_count = pno_coef.shape[2]
    slot_count = pair_occ.shape[1]
    extended = padded(pno_coef, (("blk", 0),), orbitals)
    levels = lax.broadcasted_iota(jnp.int32, (slot_count, pno_count), 1)
    pno_keep = (levels < pno_count // 4 * pno_blocks[0][:, None]).astype(jnp.float32)
    masked = amplitudes[0] * pno_keep[:, :, None] * pno_keep[:, None, :]
    lagrangian = jnp.einsum("nac,nbc->nab", masked, integrals[0], precision=lax.Precision.HIGHEST)
    slot_index = pair_offset[0] * orbitals + pair_other[0]
    owners = (pair_occ[0][:, None] == jnp.arange(orbitals, dtype=jnp.int32)[None, :]).astype(
        jnp.float32
    )
    flat_coef = pno_coef.reshape(orbitals * pno_count, basis_count)
    partner = jnp.take(extended, slot_index, axis=0)
    images = jnp.einsum("nab,nbk->nak", lagrangian, partner, precision=lax.Precision.HIGHEST)
    collected = jnp.einsum("no,nak->oak", owners, images, precision=lax.Precision.HIGHEST)
    stacked = collected.reshape(orbitals * pno_count, basis_count)
    partial_density = lax.dot_general(
        flat_coef,
        stacked,
        (((0,), (0,)), ((), ())),
        precision=lax.Precision.HIGHEST,
        preferred_element_type=jnp.float32,
    )
    return lax.psum_scatter(partial_density[None], "col", scatter_dimension=2, tiled=True)


def solution(mesh):
    in_specs = (
        P("blk", "col"),
        P("blk", "col"),
        P("blk", "col"),
        P("blk", "col"),
        P("blk", None, None),
        P("blk", "col", None, None),
        P("blk", "col", None, None),
    )
    out_specs = P("blk", None, "col")
    return jax.shard_map(local, mesh=mesh, in_specs=in_specs, out_specs=out_specs, check_vma=False)
```

profile of v0, /device:TPU:1, one launch (start us, length us, event | category | flops | bytes accessed | tf_op | source)
XLA Modules:
  0.0 175.6 jit_solution(2679031318305943885)
XLA Ops:
  6.5 0.0 copy-start
  6.5 0.0 reduce-scatter.2.cloned.1.call-start
  6.5 8.2 %collective-permute-start.1 = (f32[4,128,1024]{2,1,0:T(8,128)}, f32[4,128,1024]{2,1,0:T(8,128)S(1)}, u32[]{:S(2)}, u32[]{:S(2)}) collective-permute-start(f32[4,128,1024]{2,1,0:T(8,128)} %param.11), channel_id=1, source_target_pairs={{16,0},{32,16},{48,32},{64,48},{80,64},{96,80},{112,96},{128,112},... | collective-permute-start | bytes 6291464 | tf_op jit(solution)/shard_map/ppermute | solution.py:16
  14.8 1.9 %collective-permute-start = (f32[4,128,1024]{2,1,0:T(8,128)}, f32[4,128,1024]{2,1,0:T(8,128)S(1)}, u32[]{:S(2)}, u32[]{:S(2)}) collective-permute-start(f32[4,128,1024]{2,1,0:T(8,128)} %param.11), channel_id=1, source_target_pairs={{0,16},{16,32},{32,48},{48,64},{64,80},{80,96},{96,112},{112,128},... | collective-permute-start | bytes 6291464 | tf_op jit(solution)/shard_map/ppermute | solution.py:14
  16.7 0.7 fusion.17
  17.4 0.7 multiply_bitcast_fusion
  18.1 0.7 compare_and_fusion
  18.7 0.1 fusion.15
  18.8 0.0 copy-done
  18.8 3.5 %fusion.7 = f32[16,128,128]{2,1,0:T(8,128)S(1)} fusion(f32[1,16,128,128]{3,2,1,0:T(8,128)S(1)} %copy-done, f32[1,16,128,128]{3,2,1,0:T(8,128)} %param.12, f32[16,128]{1,0:T(8,128)S(1)} %fusion.15), kind=kOutput, calls=%fused_computation.10 | convolution fusion | flops 403177472 | bytes 3153920 | tf_op jit(solution)/shard_map/nac,nbc->nab/dot_general | solution.py:32
  22.4 37.0 %collective-permute-done.1 = f32[4,128,1024]{2,1,0:T(8,128)S(1)} collective-permute-done((f32[4,128,1024]{2,1,0:T(8,128)}, f32[4,128,1024]{2,1,0:T(8,128)S(1)}, u32[]{:S(2)}, u32[]{:S(2)}) %collective-permute-start.1) | collective-permute-done | bytes 2097184 | tf_op jit(solution)/shard_map/ppermute | solution.py:16
  59.4 7.0 %collective-permute-done = f32[4,128,1024]{2,1,0:T(8,128)S(1)} collective-permute-done((f32[4,128,1024]{2,1,0:T(8,128)}, f32[4,128,1024]{2,1,0:T(8,128)S(1)}, u32[]{:S(2)}, u32[]{:S(2)}) %collective-permute-start) | collective-permute-done | bytes 2097184 | tf_op jit(solution)/shard_map/ppermute | solution.py:14
  66.4 5.1 %pad_maximum_fusion = f32[12,128,1024]{2,1,0:T(8,128)} fusion(f32[4,128,1024]{2,1,0:T(8,128)S(1)} %collective-permute-done.1, f32[4,128,1024]{2,1,0:T(8,128)} %param.11, f32[4,128,1024]{2,1,0:T(8,128)S(1)} %collective-permute-done), kind=kLoop, calls=%fused_computation.5 | loop fusion | flops 3145728 | bytes 12582912 | tf_op jit(solution)/shard_map/concatenate | solution.py:12
  71.5 7.1 %gather_fusion = f32[16,128,1024]{2,1,0:T(8,128)} fusion(f32[12,128,1024]{2,1,0:T(8,128)} %pad_maximum_fusion, s32[1024]{0:T(1024)S(1)} %pad_clamp_fusion), kind=kCustom, calls=%fused_computation | custom fusion | bytes 16777280 | tf_op jit(solution)/shard_map/jit(_take)/gather | solution.py:38
  78.5 0.0 copy-start.2
  78.5 10.2 %fusion.2 = f32[16,128,1024]{2,1,0:T(8,128)S(1)} fusion(f32[16,128,128]{2,1,0:T(8,128)S(1)} %fusion.7, f32[16,128,1024]{2,1,0:T(8,128)} %gather_fusion, pred[16]{0:T(512)(128)(4,1)S(1)} %compare_and_fusion), kind=kOutput, calls=%fused_computation.3 | convolution fusion | flops 3223322624 | bytes 17825808 | tf_op jit(solution)/shard_map/nab,nbk->nak/dot_general | solution.py:39
  88.7 0.0 copy-start.1
  88.7 0.0 copy-done.2
  88.8 6.4 %fusion = f32[4,128,1024]{2,0,1:T(4,128)S(1)} fusion(f32[16,128,1024]{2,1,0:T(8,128)S(1)} %fusion.2, s32[16]{0:T(128)S(1)} %bitcast.28), kind=kOutput, calls=%fused_computation.1 | convolution fusion | flops 100663360 | bytes 10485824 | tf_op jit(solution)/shard_map/no,nak->oak/dot_general | solution.py:40
  95.2 0.0 copy-done.1
  95.2 10.0 %convolution_bitcast_fusion = f32[1,1024,1024]{1,2,0:T(8,128)} fusion(f32[4,128,1024]{2,1,0:T(8,128)S(1)} %copy-done.1, f32[4,128,1024]{2,0,1:T(4,128)S(1)} %fusion), kind=kOutput, calls=%fused_computation.8 | convolution fusion | flops 6442450944 | bytes 8388608 | tf_op jit(solution)/shard_map/dot_general | solution.py:42
  105.2 0.0 reduce-scatter.2.cloned.1.call-update
  105.3 63.5 %reduce-scatter.2.cloned.1.call-done = f32[1,1024,64]{1,2,0:T(8,128)} async-done(((f32[1,1024,1024]{1,2,0:T(8,128)}), f32[1,1024,64]{1,2,0:T(8,128)}) %reduce-scatter.2.cloned.1.call-update) | async-done | bytes 262160 | tf_op jit(solution)/shard_map/reduce_scatter | solution.py:49
  (1 shorter events, 0.0 us)
Async XLA Ops:
  6.5 12.3 %copy-start = (f32[1,16,128,128]{3,2,1,0:T(8,128)S(1)}, f32[1,16,128,128]{3,2,1,0:T(8,128)}, u32[]{:S(2)}) copy-start(f32[1,16,128,128]{3,2,1,0:T(8,128)} %param.13) | copy-start | bytes 3145732
  6.5 162.2 %reduce-scatter.2.cloned.1.call-start = ((), (), s32[]{:S(2)}) async-start(), calls=%async_computation.1 | async-start | bytes 4456448 | tf_op jit(solution)/shard_map/reduce_scatter | solution.py:49
  6.5 52.8 %collective-permute-start.1 = (f32[4,128,1024]{2,1,0:T(8,128)}, f32[4,128,1024]{2,1,0:T(8,128)S(1)}, u32[]{:S(2)}, u32[]{:S(2)}) collective-permute-start(f32[4,128,1024]{2,1,0:T(8,128)} %param.11), channel_id=1, source_target_pairs={{16,0},{32,16},{48,32},{64,48},{80,64},{96,80},{112,96},{128,112},... | collective-permute-start | bytes 6291464 | tf_op jit(solution)/shard_map/ppermute | solution.py:16
  14.8 51.6 %collective-permute-start = (f32[4,128,1024]{2,1,0:T(8,128)}, f32[4,128,1024]{2,1,0:T(8,128)S(1)}, u32[]{:S(2)}, u32[]{:S(2)}) collective-permute-start(f32[4,128,1024]{2,1,0:T(8,128)} %param.11), channel_id=1, source_target_pairs={{0,16},{16,32},{32,48},{48,64},{64,80},{80,96},{96,112},{112,128},... | collective-permute-start | bytes 6291464 | tf_op jit(solution)/shard_map/ppermute | solution.py:14
  78.5 10.2 %copy-start.2 = (s32[1,16]{1,0:T(1,128)S(1)}, s32[1,16]{1,0:T(1,128)}, u32[]{:S(2)}) copy-start(s32[1,16]{1,0:T(1,128)} %param.7) | copy-start | bytes 196
  88.7 6.4 %copy-start.1 = (f32[4,128,1024]{2,1,0:T(8,128)S(1)}, f32[4,128,1024]{2,1,0:T(8,128)}, u32[]{:S(2)}) copy-start(f32[4,128,1024]{2,1,0:T(8,128)} %param.11) | copy-start | bytes 6291460
Sparse Core Ops, SparseCore 0:
  105.4 63.3 reduce-scatter.1
where the time goes:
time: 178 us; the launch traced here: 176 us
  waiting for transfers between devices  108 us (61%)
  matrix products  30.1 us (17%)
  between operations  13.5 us (8%)
  starting transfers between devices  10.2 us (6%)
  other arithmetic  7.15 us (4%)
  local copies, waits for them, and re-layouts  7.11 us (4%)
    reduce_scatter x1, waiting for transfers between devices, local(): lax.psum_scatter(partial_density[None], 'col', scatter_dimension=2, tiled...  63.5 us
    ppermute x1, waiting for transfers between devices, padded(): lax.ppermute(head, axis, [((i + 1) % count, i) for i in range(count)])  37 us
    dot_general x1, matrix products, local(): jnp.einsum('nab,nbk->nak', lagrangian, partner, precision=lax.Precision.H...  10.2 us
    dot_general x1, matrix products, local(): lax.dot_general(flat_coef, stacked, (((0,), (0,)), ((), ())), precision=l...  10 us
    ppermute x1, starting transfers between devices, padded(): lax.ppermute(head, axis, [((i + 1) % count, i) for i in range(count)])  8.24 us
    gather x1, local copies, waits for them, and re-layouts, local(): partner = jnp.take(extended, slot_index, axis=0)  7.1 us
    ppermute x1, waiting for transfers between devices, padded(): lax.ppermute(tail, axis, [(i, (i + 1) % count) for i in range(count)])  7.01 us
    dot_general x1, matrix products, local(): jnp.einsum('no,nak->oak', owners, images, precision=lax.Precision.HIGHEST)  6.42 us
  transfers between devices with their start and end apart: 3, of which 3 were waited for; matrix products, arithmetic and copies ran while one was open for 3% of the time, Pallas kernels for 0%

commit v1 on v0

v1 whole, which is shorter than its diff:
```python
import jax
import jax.numpy as jnp
from jax import lax
from jax.experimental import pallas as pl
from jax.experimental.pallas import tpu as pltpu
from jax.sharding import PartitionSpec as P

F32 = jnp.float32
BF16 = jnp.bfloat16
ORB = 4
PNO = 128
AO = 1024
SLOTS = 16
CHIPS = 8
WIDE = AO // 2
NARROW = AO // 16
HALF = PNO // 2
ROWS = SLOTS * HALF
META = 8
TILES = 3 * ORB


def split(x):
    hi = x.astype(BF16)
    return hi, (x - hi.astype(F32)).astype(BF16)


def dot(a, b, dims=((1,), (0,))):
    return lax.dot_general(a, b, (dims, ((), ())), preferred_element_type=F32)


def dot3(a, b, dims=((1,), (0,))):
    return dot(a[0], b[0], dims) + (dot(a[0], b[1], dims) + dot(a[1], b[0], dims))


def select_kernel(coef_ref, out_ref):
    core = lax.axis_index("col") % 2
    first = core == 0
    left = lax.broadcasted_iota(jnp.int32, (PNO, 128), 1) < NARROW
    for k in range(CHIPS // 2):
        a = coef_ref[0, :, 256 * k : 256 * k + 128]
        b = coef_ref[0, :, 256 * k + 128 : 256 * k + 256]
        moved = pltpu.roll(jnp.where(first, b, a), NARROW, 1)
        out_ref[:, 128 * k : 128 * k + 128] = jnp.where(
            left, jnp.where(first, a, moved), jnp.where(first, moved, b)
        )


def lagrangian_kernel(occ_ref, offset_ref, other_ref, blocks_ref, amp_ref, int_ref, keep_ref, send_ref):
    upper = (lax.axis_index("col") // 2) % 2 == 1
    rows = lax.broadcasted_iota(jnp.int32, (PNO, PNO), 0)
    cols = lax.broadcasted_iota(jnp.int32, (PNO, PNO), 1)
    far = jnp.maximum(rows, cols)
    lane = lax.broadcasted_iota(jnp.int32, (META, 128), 1)
    meta = jnp.zeros((META, 128), F32)
    for p in range(SLOTS):
        kept = jnp.where(far < PNO // 4 * blocks_ref[0, p], amp_ref[0, p], 0.0)
        lag = dot3(split(kept), split(int_ref[0, p]), ((1,), (1,)))
        low, high = lag[:HALF], lag[HALF:]
        keep_ref[p * HALF : (p + 1) * HALF, :] = jnp.where(upper, high, low)
        send_ref[p * HALF : (p + 1) * HALF, :] = jnp.where(upper, low, high)
        block = (offset_ref[0, p] * ORB + other_ref[0, p]) * ORB + occ_ref[0, p]
        meta = jnp.where(lane == p, block.astype(F32), meta)
    keep_ref[ROWS:, :] = meta
    send_ref[ROWS:, :] = meta


def gather_kernel(m0, m1, m2, m3, l0, l1, l2, l3, x_ref, hi_ref, lo_ref, same_ref, block_ref):
    block_ref[...] = jnp.zeros_like(block_ref)
    for meta_ref, lag_ref in ((m0, l0), (m1, l1), (m2, l2), (m3, l3)):
        for p in range(SLOTS):
            number = meta_ref[0, p].astype(jnp.int32)
            block_ref[number] += lag_ref[p * HALF : (p + 1) * HALF, :]
    for side, first in enumerate((0, 2 * ORB)):
        for j in range(ORB):
            for o in range(ORB):
                hi, lo = split(block_ref[(first + j) * ORB + o])
                at = (slice(o * HALF, (o + 1) * HALF), slice((side * ORB + j) * PNO, (side * ORB + j + 1) * PNO))
                hi_ref[at] = hi
                lo_ref[at] = lo
    total = jnp.zeros((ORB * HALF, WIDE), F32)
    for j in range(ORB):
        lhs = jnp.concatenate([block_ref[(ORB + j) * ORB + o] for o in range(ORB)], axis=0)
        total += dot3(split(lhs), split(x_ref[j * PNO : (j + 1) * PNO, :]))
    same_ref[...] = total


def images_kernel(hi_ref, lo_ref, same_ref, prev_ref, next_ref, out_ref):
    total = same_ref[...]
    for side, x_ref in enumerate((prev_ref, next_ref)):
        x = split(x_ref[...])
        at = slice(side * ORB * PNO, (side + 1) * ORB * PNO)
        total += dot3((hi_ref[:, at], lo_ref[:, at]), x)
    left = lax.broadcasted_iota(jnp.int32, (2 * HALF, 128), 1) < NARROW
    for k in range(CHIPS // 2):
        top = total[: 2 * HALF, 128 * k : 128 * k + 128]
        low = total[2 * HALF :, 128 * k : 128 * k + 128]
        out_ref[2 * k] = jnp.where(left, top, pltpu.roll(low, NARROW, 1))
        out_ref[2 * k + 1] = jnp.where(left, pltpu.roll(top, NARROW, 1), low)


def density_kernel(part_ref, coef_ref, out_ref):
    sums = []
    for h in range(2):
        s = (part_ref[h] + part_ref[h + 2]) + (part_ref[h + 4] + part_ref[h + 6])
        sums.append(s.T)
    total = jnp.zeros((NARROW, AO), F32)
    for pair in range(2):
        lhs = jnp.concatenate([s[NARROW * pair : NARROW * (pair + 1)] for s in sums], axis=1)
        rhs = jnp.concatenate(
            [
                coef_ref[2 * pair + o, HALF * h : HALF * (h + 1), :]
                for h in range(2)
                for o in range(2)
            ],
            axis=0,
        )
        total += dot3(split(lhs), split(rhs))
    out_ref[...] = total


def cost(macs, size):
    return pl.CostEstimate(flops=2 * macs, bytes_accessed=size, transcendentals=0)


PARAMS = pltpu.CompilerParams(vmem_limit_bytes=48 * 1024 * 1024)


def local(pair_occ, pair_offset, pair_other, pno_blocks, pno_coef, amplitudes, integrals):
    smem = pl.BlockSpec(memory_space=pltpu.SMEM)
    tiles = lax.axis_size("blk")
    devices = lax.axis_size("col")

    own = pl.pallas_call(
        select_kernel,
        grid=(ORB,),
        in_specs=[pl.BlockSpec((1, PNO, AO), lambda i: (i, 0, 0))],
        out_specs=pl.BlockSpec((PNO, WIDE), lambda i: (i, 0)),
        out_shape=jax.ShapeDtypeStruct((ORB * PNO, WIDE), F32),
        compiler_params=PARAMS,
        cost_estimate=cost(0, 3 << 20),
        name="select",
    )(pno_coef)
    prev = lax.ppermute(own, "blk", [(i, (i + 1) % tiles) for i in range(tiles)])
    succ = lax.ppermute(own, "blk", [((i + 1) % tiles, i) for i in range(tiles)])

    half = jax.ShapeDtypeStruct((ROWS + META, 128), F32)
    keep, send = pl.pallas_call(
        lagrangian_kernel,
        in_specs=[smem] * 4 + [pl.BlockSpec(memory_space=pltpu.VMEM)] * 2,
        out_shape=(half, half),
        compiler_params=PARAMS,
        cost_estimate=cost(3 * SLOTS * PNO**3, 3 << 20),
        name="lagrangian",
    )(pair_occ, pair_offset, pair_other, pno_blocks, amplitudes, integrals)

    swap = lambda x, bit: lax.ppermute(x, "col", [(i, i ^ bit) for i in range(devices)])
    far = swap(send, 2)
    halves = (keep, far, swap(keep, 1), swap(far, 1))
    meta = pl.BlockSpec((META, 128), lambda i: (ROWS // META, 0), memory_space=pltpu.SMEM)
    body = pl.BlockSpec((ROWS, 128), lambda i: (0, 0))
    whole = lambda *shape: pl.BlockSpec(shape, lambda i: (0,) * len(shape))
    wide = 2 * ORB * PNO
    hi, lo, same = pl.pallas_call(
        gather_kernel,
        grid=(1,),
        in_specs=[meta] * 4 + [body] * 4 + [whole(ORB * PNO, WIDE)],
        out_specs=[whole(ORB * HALF, wide), whole(ORB * HALF, wide), whole(ORB * HALF, WIDE)],
        out_shape=(
            jax.ShapeDtypeStruct((ORB * HALF, wide), BF16),
            jax.ShapeDtypeStruct((ORB * HALF, wide), BF16),
            jax.ShapeDtypeStruct((ORB * HALF, WIDE), F32),
        ),
        scratch_shapes=[pltpu.VMEM((TILES * ORB, HALF, PNO), F32)],
        compiler_params=PARAMS,
        cost_estimate=cost(3 * ORB * HALF * ORB * PNO * WIDE, 4 << 20),
        name="gather",
    )(*halves, *halves, own)

    parts = pl.pallas_call(
        images_kernel,
        out_shape=jax.ShapeDtypeStruct((CHIPS, 2 * HALF, 128), F32),
        compiler_params=PARAMS,
        cost_estimate=cost(3 * ORB * HALF * wide * WIDE, 4 << 20),
        name="images",
    )(hi, lo, same, prev, succ)
    groups = [[2 * z + c for z in range(CHIPS)] for c in range(2)]
    parts = lax.all_to_all(parts, "col", 0, 0, axis_index_groups=groups)

    out = pl.pallas_call(
        density_kernel,
        out_shape=jax.ShapeDtypeStruct((NARROW, AO), F32),
        compiler_params=PARAMS,
        cost_estimate=cost(3 * ORB * PNO * NARROW * AO, 3 << 20),
        name="density",
    )(parts, pno_coef)
    return out.T[None]


def solution(mesh):
    in_specs = (
        P("blk", "col"),
        P("blk", "col"),
        P("blk", "col"),
        P("blk", "col"),
        P("blk", None, None),
        P("blk", "col", None, None),
        P("blk", "col", None, None),
    )
    out_specs = P("blk", None, "col")
    return jax.shard_map(local, mesh=mesh, in_specs=in_specs, out_specs=out_specs, check_vma=False)
```

time: 178 us -> 75.3 us (0.42)
  waiting for transfers between devices: 108 us -> 19 us
  matrix products: 30.1 us -> 0 us
  blocking collectives: 0 us -> 23.4 us
  between operations: 13.5 us -> 0.1 us
  starting transfers between devices: 10.2 us -> 19.2 us
  Pallas kernels: 0 us -> 7.55 us
  other arithmetic: 7.15 us -> 0 us
  local copies, waits for them, and re-layouts: 7.11 us -> 5.07 us
    reduce_scatter x1 -> x0, waiting for transfers between devices: 63.5 us -> none  [local(): lax.psum_scatter(partial_density[None], 'col', scatter_dimension=2, tiled...]
    dot_general x4 -> x0, matrix products: 30.1 us -> none  [the longest x1 10.2 us: local(): jnp.einsum('nab,nbk->nak', lagrangian, partner, precision=lax.Precision.H...]
    ppermute x2 -> x5, waiting for transfers between devices: 44 us -> 19 us  [the longest x1 10.1 us: local(): lax.ppermute(own, 'blk', [((i + 1) % tiles, i) for i in range(tiles)])]
    all_to_all x0 -> x1, blocking collectives: none -> 23.4 us  [local(): parts = lax.all_to_all(parts, 'col', 0, 0, axis_index_groups=groups)]
    ppermute x2 -> x5, starting transfers between devices: 10.2 us -> 19.2 us  [the longest x3 9.98 us: local(): lax.ppermute(x, 'col', [(i, i ^ bit) for i in range(devices)])]
    pallas_call x0 -> x5, Pallas kernels: none -> 7.55 us  [the longest x1 2.52 us: local(): pl.pallas_call(gather_kernel, grid=(1,), in_specs=[meta] * 4 + [body] * 4...]
    gather x1 -> x0, local copies, waits for them, and re-layouts: 7.1 us -> none  [local(): partner = jnp.take(extended, slot_index, axis=0)]
    unnamed x6 -> x14, local copies, waits for them, and re-layouts: 0.01 us -> 5.07 us
  transfers between devices with their start and end apart: 3 -> 5, of which waited for: 3 -> 3; matrix products, arithmetic and copies ran while one was open for 3% -> 0% of each run, Pallas kernels for 0% -> 4%
where the time goes in v1:
time: 75.3 us; the launch traced here: 74.3 us
  blocking collectives  23.4 us (31%)
  starting transfers between devices  19.2 us (25%)
  waiting for transfers between devices  19 us (25%)
  Pallas kernels  7.55 us (10%)
  local copies, waits for them, and re-layouts  5.07 us (7%)
    all_to_all x1, blocking collectives, local(): parts = lax.all_to_all(parts, 'col', 0, 0, axis_index_groups=groups)  23.4 us
    ppermute x1, waiting for transfers between devices, local(): lax.ppermute(own, 'blk', [((i + 1) % tiles, i) for i in range(tiles)])  10.1 us
    ppermute x3, starting transfers between devices, local(): lax.ppermute(x, 'col', [(i, i ^ bit) for i in range(devices)])  9.98 us
    ppermute x1, starting transfers between devices, local(): lax.ppermute(own, 'blk', [((i + 1) % tiles, i) for i in range(tiles)])  7.29 us
    ppermute x1, waiting for transfers between devices, local(): lax.ppermute(own, 'blk', [(i, (i + 1) % tiles) for i in range(tiles)])  7.15 us
    unnamed x14, local copies, waits for them, and re-layouts  5.07 us
    pallas_call x1, Pallas kernels, local(): pl.pallas_call(gather_kernel, grid=(1,), in_specs=[meta] * 4 + [body] * 4...  2.52 us
    ppermute x1, starting transfers between devices, local(): lax.ppermute(own, 'blk', [(i, (i + 1) % tiles) for i in range(tiles)])  1.92 us
  transfers between devices with their start and end apart: 5, of which 3 were waited for; matrix products, arithmetic and copies ran while one was open for 0% of the time, Pallas kernels for 4%

profile of v1, /device:TPU:1, one launch (start us, length us, event | category | flops | bytes accessed | tf_op | source)
XLA Modules:
  0.0 74.3 jit_solution(9348985069408464998)
XLA Ops:
  0.0 0.0 copy-start.1
  0.0 1.2 %copy-done.1 = f32[1,16,128,128]{3,2,1,0:T(8,128)S(1)} copy-done((f32[1,16,128,128]{3,2,1,0:T(8,128)S(1)}, f32[1,16,128,128]{3,2,1,0:T(8,128)}, u32[]{:S(2)}) %copy-start.1) | copy-done | bytes 1048600
  1.2 0.0 copy-start.2
  1.2 1.2 %copy-done.2 = f32[1,16,128,128]{3,2,1,0:T(8,128)S(1)} copy-done((f32[1,16,128,128]{3,2,1,0:T(8,128)S(1)}, f32[1,16,128,128]{3,2,1,0:T(8,128)}, u32[]{:S(2)}) %copy-start.2) | copy-done | bytes 1048600
  2.5 0.0 copy-start.3
  2.5 0.7 copy-done.3
  3.1 0.0 copy-start.4
  3.1 0.7 copy-done.4
  3.8 0.0 copy-start.5
  3.8 0.7 copy-done.5
  4.4 0.0 copy-start.6
  4.4 0.7 copy-done.6
  5.1 0.0 copy-start
  5.1 1.8 %lagrangian.1 = (f32[1032,128]{1,0:T(8,128)S(1)}, f32[1032,128]{1,0:T(8,128)S(1)}) custom-call(s32[1,16]{1,0:T(1,128)S(1)} %copy-done.3, s32[1,16]{1,0:T(1,128)S(1)} %copy-done.4, s32[1,16]{1,0:T(1,128)S(1)} %copy-done.5, s32[1,16]{1,0:T(1,128)S(1)} %copy-done.6, f32[1,16,128,128]{3,2,1,0:T(8,128)S(1)} %copy-done.1, f32[1,16,128,128]{3,2,1,0:T(8,128)S(1)} %copy-done.2), custom_call_target="tpu_custom_call" | custom-call | flops 201326592 | bytes 3145728 | tf_op jit(solution)/shard_map/lagrangian/pallas_call | solution.py:148
  6.8 4.8 %collective-permute-start = (f32[1032,128]{1,0:T(8,128)S(1)}, f32[1032,128]{1,0:T(8,128)S(1)}, u32[]{:S(2)}, u32[]{:S(2)}) collective-permute-start(f32[1032,128]{1,0:T(8,128)S(1)} %get-tuple-element.11), channel_id=1, source_target_pairs={{0,2},{1,3},{2,0},{3,1},{4,6},{5,7},{6,4},{7,5},{8,10},{9,11},{10,... | collective-permute-start | bytes 1585160 | tf_op jit(solution)/shard_map/ppermute | solution.py:157
  11.7 0.0 copy-done
  11.7 0.6 select.1.x_ref
  12.3 7.3 %collective-permute-start.4 = (f32[512,512]{1,0:T(8,128)S(1)}, f32[512,512]{1,0:T(8,128)S(1)}, u32[]{:S(2)}, u32[]{:S(2)}) collective-permute-start(f32[512,512]{1,0:T(8,128)S(1)} %select.1.x_ref), channel_id=1, source_target_pairs={{16,0},{32,16},{48,32},{64,48},{80,64},{96,80},{112,96},{128,112},... | collective-permute-start | bytes 3145736 | tf_op jit(solution)/shard_map/ppermute | solution.py:145
  19.6 1.9 %collective-permute-start.3 = (f32[512,512]{1,0:T(8,128)S(1)}, f32[512,512]{1,0:T(8,128)S(1)}, u32[]{:S(2)}, u32[]{:S(2)}) collective-permute-start(f32[512,512]{1,0:T(8,128)S(1)} %select.1.x_ref), channel_id=1, source_target_pairs={{0,16},{16,32},{32,48},{48,64},{64,80},{80,96},{96,112},{112,128},... | collective-permute-start | bytes 3145736 | tf_op jit(solution)/shard_map/ppermute | solution.py:144
  21.6 3.1 %collective-permute-start.1 = (f32[1032,128]{1,0:T(8,128)S(1)}, f32[1032,128]{1,0:T(8,128)S(1)}, u32[]{:S(2)}, u32[]{:S(2)}) collective-permute-start(f32[1032,128]{1,0:T(8,128)S(1)} %get-tuple-element.10.m0.l0), channel_id=1, source_target_pairs={{0,1},{1,0},{2,3},{3,2},{4,5},{5,4},{6,7},{7,6},{8,9},{9,8},{10,11... | collective-permute-start | bytes 1585160 | tf_op jit(solution)/shard_map/ppermute | solution.py:157
  24.7 0.0 collective-permute-done.m1.l1
  24.7 2.0 %collective-permute-start.2 = (f32[1032,128]{1,0:T(8,128)S(1)}, f32[1032,128]{1,0:T(8,128)S(1)}, u32[]{:S(2)}, u32[]{:S(2)}) collective-permute-start(f32[1032,128]{1,0:T(8,128)S(1)} %collective-permute-done.m1.l1), channel_id=1, source_target_pairs={{0,1},{1,0},{2,3},{3,2},{4,5},{5,4},{6,7},{7,6},{8,9},{9,8},{10,11... | collective-permute-start | bytes 1585160 | tf_op jit(solution)/shard_map/ppermute | solution.py:157
  26.7 0.0 collective-permute-done.1.m2.l2
  26.8 1.8 %collective-permute-done.2.m3.l3 = f32[1032,128]{1,0:T(8,128)S(1)} collective-permute-done((f32[1032,128]{1,0:T(8,128)S(1)}, f32[1032,128]{1,0:T(8,128)S(1)}, u32[]{:S(2)}, u32[]{:S(2)}) %collective-permute-start.2) | collective-permute-done | bytes 528416 | tf_op jit(solution)/shard_map/ppermute | solution.py:157
  28.5 2.5 %gather.1 = (bf16[256,1024]{1,0:T(8,128)(2,1)S(1)}, bf16[256,1024]{1,0:T(8,128)(2,1)S(1)}, f32[256,512]{1,0:T(8,128)S(1)}) custom-call(f32[1032,128]{1,0:T(8,128)S(1)} %get-tuple-element.10.m0.l0, f32[1032,128]{1,0:T(8,128)S(1)} %collective-permute-done.m1.l1, f32[1032,128]{1,0:T(8,128)S(1)} %collective-permute-done.1.m2.l2, ...), custom_call_target="tpu_custom_call" | custom-call | flops 402653184 | bytes 4194304 | tf_op jit(solution)/shard_map/gather/pallas_call | solution.py:164
  31.1 10.1 %collective-permute-done.4.next_ref = f32[512,512]{1,0:T(8,128)S(1)} collective-permute-done((f32[512,512]{1,0:T(8,128)S(1)}, f32[512,512]{1,0:T(8,128)S(1)}, u32[]{:S(2)}, u32[]{:S(2)}) %collective-permute-start.4) | collective-permute-done | bytes 1048608 | tf_op jit(solution)/shard_map/ppermute | solution.py:145
  41.1 7.1 %collective-permute-done.3.prev_ref = f32[512,512]{1,0:T(8,128)S(1)} collective-permute-done((f32[512,512]{1,0:T(8,128)S(1)}, f32[512,512]{1,0:T(8,128)S(1)}, u32[]{:S(2)}, u32[]{:S(2)}) %collective-permute-start.3) | collective-permute-done | bytes 1048608 | tf_op jit(solution)/shard_map/ppermute | solution.py:144
  48.3 1.2 %images.1 = f32[8,128,128]{2,1,0:T(8,128)S(1)} custom-call(bf16[256,1024]{1,0:T(8,128)(2,1)S(1)} %get-tuple-element.12.hi_ref, bf16[256,1024]{1,0:T(8,128)(2,1)S(1)} %get-tuple-element.13.lo_ref, f32[256,512]{1,0:T(8,128)S(1)} %get-tuple-element.14.same_ref, f32[512,512]{1,0:T(8,128)S(1)} %collective-permute-done.3.prev_ref, ...), custom_call_target="tpu_custom_call" | custom-call | flops 805306368 | bytes 4194304 | tf_op jit(solution)/shard_map/images/pallas_call | solution.py:180
  49.5 23.4 %all_to_all.5.part_ref = f32[8,128,128]{2,1,0:T(8,128)S(1)} all-to-all(f32[8,128,128]{2,1,0:T(8,128)S(1)} %images.1), channel_id=1, replica_groups={{0,2,4,6,8,10,12,14},{1,3,5,7,9,11,13,15},{16,18,20,22,24,26,28,30},{17..., dimensions={0} | all-to-all | bytes 1048576 | tf_op jit(solution)/shard_map/all_to_all | solution.py:188
  72.8 1.4 %density.1 = f32[64,1024]{1,0:T(8,128)} custom-call(f32[8,128,128]{2,1,0:T(8,128)S(1)} %all_to_all.5.part_ref, f32[4,128,1024]{2,1,0:T(8,128)S(1)} %copy-done), custom_call_target="tpu_custom_call" | custom-call | flops 201326592 | bytes 3145728 | tf_op jit(solution)/shard_map/density/pallas_call | solution.py:190
Async XLA Ops:
  0.0 1.2 %copy-start.1 = (f32[1,16,128,128]{3,2,1,0:T(8,128)S(1)}, f32[1,16,128,128]{3,2,1,0:T(8,128)}, u32[]{:S(2)}) copy-start(f32[1,16,128,128]{3,2,1,0:T(8,128)} %amp_ref.1) | copy-start | bytes 3145732
  1.2 1.2 %copy-start.2 = (f32[1,16,128,128]{3,2,1,0:T(8,128)S(1)}, f32[1,16,128,128]{3,2,1,0:T(8,128)}, u32[]{:S(2)}) copy-start(f32[1,16,128,128]{3,2,1,0:T(8,128)} %int_ref.1) | copy-start | bytes 3145732
  2.5 0.7 copy-start.3
  3.1 0.7 copy-start.4
  3.8 0.7 copy-start.5
  4.4 0.7 copy-start.6
  5.1 6.6 %copy-start = (f32[4,128,1024]{2,1,0:T(8,128)S(1)}, f32[4,128,1024]{2,1,0:T(8,128)}, u32[]{:S(2)}) copy-start(f32[4,128,1024]{2,1,0:T(8,128)} %coef_ref.3) | copy-start | bytes 6291460
  6.8 17.9 %collective-permute-start = (f32[1032,128]{1,0:T(8,128)S(1)}, f32[1032,128]{1,0:T(8,128)S(1)}, u32[]{:S(2)}, u32[]{:S(2)}) collective-permute-start(f32[1032,128]{1,0:T(8,128)S(1)} %get-tuple-element.11), channel_id=1, source_target_pairs={{0,2},{1,3},{2,0},{3,1},{4,6},{5,7},{6,4},{7,5},{8,10},{9,11},{10,... | collective-permute-start | bytes 1585160 | tf_op jit(solution)/shard_map/ppermute | solution.py:157
  12.3 28.8 %collective-permute-start.4 = (f32[512,512]{1,0:T(8,128)S(1)}, f32[512,512]{1,0:T(8,128)S(1)}, u32[]{:S(2)}, u32[]{:S(2)}) collective-permute-start(f32[512,512]{1,0:T(8,128)S(1)} %select.1.x_ref), channel_id=1, source_target_pairs={{16,0},{32,16},{48,32},{64,48},{80,64},{96,80},{112,96},{128,112},... | collective-permute-start | bytes 3145736 | tf_op jit(solution)/shard_map/ppermute | solution.py:145
  19.6 28.6 %collective-permute-start.3 = (f32[512,512]{1,0:T(8,128)S(1)}, f32[512,512]{1,0:T(8,128)S(1)}, u32[]{:S(2)}, u32[]{:S(2)}) collective-permute-start(f32[512,512]{1,0:T(8,128)S(1)} %select.1.x_ref), channel_id=1, source_target_pairs={{0,16},{16,32},{32,48},{48,64},{64,80},{80,96},{96,112},{112,128},... | collective-permute-start | bytes 3145736 | tf_op jit(solution)/shard_map/ppermute | solution.py:144
  21.6 5.2 %collective-permute-start.1 = (f32[1032,128]{1,0:T(8,128)S(1)}, f32[1032,128]{1,0:T(8,128)S(1)}, u32[]{:S(2)}, u32[]{:S(2)}) collective-permute-start(f32[1032,128]{1,0:T(8,128)S(1)} %get-tuple-element.10.m0.l0), channel_id=1, source_target_pairs={{0,1},{1,0},{2,3},{3,2},{4,5},{5,4},{6,7},{7,6},{8,9},{9,8},{10,11... | collective-permute-start | bytes 1585160 | tf_op jit(solution)/shard_map/ppermute | solution.py:157
  24.7 3.8 %collective-permute-start.2 = (f32[1032,128]{1,0:T(8,128)S(1)}, f32[1032,128]{1,0:T(8,128)S(1)}, u32[]{:S(2)}, u32[]{:S(2)}) collective-permute-start(f32[1032,128]{1,0:T(8,128)S(1)} %collective-permute-done.m1.l1), channel_id=1, source_target_pairs={{0,1},{1,0},{2,3},{3,2},{4,5},{5,4},{6,7},{7,6},{8,9},{9,8},{10,11... | collective-permute-start | bytes 1585160 | tf_op jit(solution)/shard_map/ppermute | solution.py:157

commit v2 on v1

v2 whole, which is shorter than its diff:
```python
import jax
import jax.numpy as jnp
from jax import lax
from jax.experimental import pallas as pl
from jax.experimental.pallas import tpu as pltpu
from jax.sharding import PartitionSpec as P

F32 = jnp.float32
BF16 = jnp.bfloat16
ORB = 4
PNO = 128
AO = 1024
SLOTS = 16
CHIPS = 8
WIDE = AO // 2
NARROW = AO // 16
HALF = PNO // 2
ROWS = SLOTS * HALF
META = 8
TILES = 3 * ORB


def split(x):
    hi = x.astype(BF16)
    return hi, (x - hi.astype(F32)).astype(BF16)


def dot(a, b, dims=((1,), (0,))):
    return lax.dot_general(a, b, (dims, ((), ())), preferred_element_type=F32)


def dot3(a, b, dims=((1,), (0,))):
    return dot(a[0], b[0], dims) + (dot(a[0], b[1], dims) + dot(a[1], b[0], dims))


def select_kernel(occ_ref, offset_ref, other_ref, blocks_ref, coef_ref, out_ref, meta_ref, keep_ref, held, numbers, sems):
    copies = [
        pltpu.make_async_copy(coef_ref.at[o, pl.ds(h * HALF, HALF)], held.at[o, pl.ds(h * HALF, HALF)], sems.at[o * 2 + h])
        for o in range(ORB)
        for h in range(2)
    ]
    lists = [
        pltpu.make_async_copy(ref, numbers.at[pl.ds(i, 1)], sems.at[2 * ORB + i])
        for i, ref in enumerate((occ_ref, offset_ref, other_ref, blocks_ref))
    ]
    for copy in lists + copies:
        copy.start()
    for copy in lists:
        copy.wait()
    lane = lax.broadcasted_iota(jnp.int32, (META, 128), 1)
    meta = jnp.zeros((META, 128), jnp.int32)
    for p in range(SLOTS):
        block = (numbers[1, p] * ORB + numbers[2, p]) * ORB + numbers[0, p]
        meta = jnp.where(lane == p, block, meta)
        keep_ref[p] = jnp.full((8, 128), PNO // 4 * numbers[3, p], jnp.int32)
    meta_ref[...] = meta.astype(F32)
    first = lax.axis_index("col") % 2 == 0
    left = lax.broadcasted_iota(jnp.int32, (HALF, 128), 1) < NARROW
    for i, copy in enumerate(copies):
        copy.wait()
        rows = slice(i % 2 * HALF, (i % 2 + 1) * HALF)
        for k in range(CHIPS // 2):
            a = held[i // 2, rows, 256 * k : 256 * k + 128]
            b = held[i // 2, rows, 256 * k + 128 : 256 * k + 256]
            moved = pltpu.roll(jnp.where(first, b, a), NARROW, 1)
            out_ref[i * HALF : (i + 1) * HALF, 128 * k : 128 * k + 128] = jnp.where(
                left, jnp.where(first, a, moved), jnp.where(first, moved, b)
            )


def lagrangian_kernel(meta_ref, kept_ref, amp_ref, int_ref, keep_ref, send_ref):
    upper = (lax.axis_index("col") // 2) % 2 == 1
    far = jnp.maximum(
        lax.broadcasted_iota(jnp.int32, (PNO, PNO), 0), lax.broadcasted_iota(jnp.int32, (PNO, PNO), 1)
    )
    for p in range(SLOTS):
        kept = jnp.where(far < kept_ref[p, 0:1, :], amp_ref[0, p], 0.0)
        lag = dot3(split(kept), split(int_ref[0, p]), ((1,), (1,)))
        low, high = lag[:HALF], lag[HALF:]
        at = slice(p * HALF, (p + 1) * HALF)
        keep_ref[at, :] = jnp.where(upper, high, low)
        send_ref[at, :] = jnp.where(upper, low, high)
    keep_ref[ROWS:, :] = meta_ref[...]
    send_ref[ROWS:, :] = meta_ref[...]


def add_slots(block_ref, meta_ref, lag_ref):
    for p in range(SLOTS):
        number = meta_ref[0, p].astype(jnp.int32)
        block_ref[number] += lag_ref[p * HALF : (p + 1) * HALF, :]


def gather_kernel(m0, m1, m2, l0, l1, l2, block_ref):
    block_ref[...] = jnp.zeros_like(block_ref)
    add_slots(block_ref, m0, l0)
    add_slots(block_ref, m1, l1)
    add_slots(block_ref, m2, l2)


def images_kernel(meta_ref, lag_ref, some_ref, prev_ref, own_ref, next_ref, out_ref, block_ref):
    add_slots(block_ref, meta_ref, lag_ref)
    total = jnp.zeros((ORB * HALF, WIDE), F32)
    for side, x_ref in enumerate((prev_ref, own_ref, next_ref)):
        for j in range(0, ORB, 2):
            lhs = jnp.concatenate(
                [
                    jnp.concatenate([block_ref[(side * ORB + j + i) * ORB + o] for i in range(2)], axis=1)
                    for o in range(ORB)
                ],
                axis=0,
            )
            total += dot3(split(lhs), split(x_ref[j * PNO : (j + 2) * PNO, :]))
    left = lax.broadcasted_iota(jnp.int32, (2 * HALF, 128), 1) < NARROW
    for k in range(CHIPS // 2):
        top = total[: 2 * HALF, 128 * k : 128 * k + 128]
        low = total[2 * HALF :, 128 * k : 128 * k + 128]
        out_ref[2 * k] = jnp.where(left, top, pltpu.roll(low, NARROW, 1))
        out_ref[2 * k + 1] = jnp.where(left, pltpu.roll(top, NARROW, 1), low)


def density_kernel(part_ref, coef_ref, out_ref):
    sums = []
    for h in range(2):
        s = (part_ref[h] + part_ref[h + 2]) + (part_ref[h + 4] + part_ref[h + 6])
        sums.append(s.T)
    total = jnp.zeros((NARROW, AO), F32)
    for pair in range(2):
        lhs = jnp.concatenate([s[NARROW * pair : NARROW * (pair + 1)] for s in sums], axis=1)
        rhs = jnp.concatenate(
            [coef_ref[2 * pair + o, HALF * h : HALF * (h + 1), :] for h in range(2) for o in range(2)],
            axis=0,
        )
        total += dot3(split(lhs), split(rhs))
    out_ref[...] = total


def cost(macs, size):
    return pl.CostEstimate(flops=2 * macs, bytes_accessed=size, transcendentals=0)


PARAMS = pltpu.CompilerParams(vmem_limit_bytes=48 * 1024 * 1024)


def local(pair_occ, pair_offset, pair_other, pno_blocks, pno_coef, amplitudes, integrals):
    tiles = lax.axis_size("blk")
    devices = lax.axis_size("col")
    whole = lambda *shape: pl.BlockSpec(shape, lambda i: (0,) * len(shape))
    in_place = lambda x: pltpu.with_memory_space_constraint(x, pltpu.HBM)

    own, numbers, kept = pl.pallas_call(
        select_kernel,
        in_specs=[pl.BlockSpec(memory_space=pltpu.HBM)] * 5,
        out_shape=(
            jax.ShapeDtypeStruct((ORB * PNO, WIDE), F32),
            jax.ShapeDtypeStruct((META, 128), F32),
            jax.ShapeDtypeStruct((SLOTS, 8, 128), jnp.int32),
        ),
        scratch_shapes=[
            pltpu.VMEM((ORB, PNO, AO), F32),
            pltpu.SMEM((4, SLOTS), jnp.int32),
            pltpu.SemaphoreType.DMA((2 * ORB + 4,)),
        ],
        compiler_params=PARAMS,
        cost_estimate=cost(0, 3 << 20),
        name="select",
    )(*map(in_place, (pair_occ, pair_offset, pair_other, pno_blocks, pno_coef)))
    prev = lax.ppermute(own, "blk", [(i, (i + 1) % tiles) for i in range(tiles)])
    succ = lax.ppermute(own, "blk", [((i + 1) % tiles, i) for i in range(tiles)])

    half = jax.ShapeDtypeStruct((ROWS + META, 128), F32)
    keep, send = pl.pallas_call(
        lagrangian_kernel,
        out_shape=(half, half),
        compiler_params=PARAMS,
        cost_estimate=cost(3 * SLOTS * PNO**3, 3 << 20),
        name="lagrangian",
    )(numbers, kept, amplitudes, integrals)

    swap = lambda x, bit: lax.ppermute(x, "col", [(i, i ^ bit) for i in range(devices)])
    far, near = lax.cond(
        pno_blocks[0, 0] > 0,
        lambda keep, send: (swap(send, 2), swap(keep, 1)),
        lambda keep, send: (jnp.zeros_like(send), jnp.zeros_like(keep)),
        *(keep, send),
    )
    last = swap(far, 1)

    meta = pl.BlockSpec((META, 128), lambda i: (ROWS // META, 0), memory_space=pltpu.SMEM)
    body = pl.BlockSpec((ROWS, 128), lambda i: (0, 0))
    blocks = (TILES * ORB, HALF, PNO)
    some = pl.pallas_call(
        gather_kernel,
        grid=(1,),
        in_specs=[meta] * 3 + [body] * 3,
        out_specs=whole(*blocks),
        out_shape=jax.ShapeDtypeStruct(blocks, F32),
        compiler_params=PARAMS,
        cost_estimate=cost(0, 0),
        name="gather",
    )(keep, near, far, keep, near, far)
    tile = whole(ORB * PNO, WIDE)
    parts, _ = pl.pallas_call(
        images_kernel,
        grid=(1,),
        in_specs=[meta, body, whole(*blocks), tile, tile, tile],
        out_specs=[whole(CHIPS, 2 * HALF, 128), whole(*blocks)],
        out_shape=(
            jax.ShapeDtypeStruct((CHIPS, 2 * HALF, 128), F32),
            jax.ShapeDtypeStruct(blocks, F32),
        ),
        input_output_aliases={2: 1},
        compiler_params=PARAMS,
        cost_estimate=cost(3 * ORB * HALF * TILES * PNO * WIDE, 4 << 20),
        name="images",
    )(last, last, some, prev, own, succ)
    groups = [[2 * z + c for z in range(CHIPS)] for c in range(2)]
    parts = lax.all_to_all(parts, "col", 0, 0, axis_index_groups=groups)

    out = pl.pallas_call(
        density_kernel,
        out_shape=jax.ShapeDtypeStruct((NARROW, AO), F32),
        compiler_params=PARAMS,
        cost_estimate=cost(3 * ORB * PNO * NARROW * AO, 3 << 20),
        name="density",
    )(parts, pno_coef)
    return out.T[None]


def solution(mesh):
    in_specs = (
        P("blk", "col"),
        P("blk", "col"),
        P("blk", "col"),
        P("blk", "col"),
        P("blk", None, None),
        P("blk", "col", None, None),
        P("blk", "col", None, None),
    )
    out_specs = P("blk", None, "col")
    return jax.shard_map(local, mesh=mesh, in_specs=in_specs, out_specs=out_specs, check_vma=False)
```

time: 75.3 us -> 68.1 us (0.904)
  waiting for transfers between devices: 19 us -> 11.4 us
  local copies, waits for them, and re-layouts: 5.07 us -> 0.81 us
  starting transfers between devices: 19.2 us -> 21.8 us
  Pallas kernels: 7.55 us -> 8.76 us
  blocking collectives: 23.4 us -> 24.4 us
    ppermute x1, waiting for transfers between devices: 10.1 us -> 0.01 us  [local(): lax.ppermute(own, 'blk', [((i + 1) % tiles, i) for i in range(tiles)])]
    ppermute x3, waiting for transfers between devices: 1.78 us -> 7.19 us  [local(): lax.ppermute(x, 'col', [(i, i ^ bit) for i in range(devices)])]
    unnamed x14 -> x10, local copies, waits for them, and re-layouts: 5.07 us -> 0.81 us
    ppermute x1, waiting for transfers between devices: 7.15 us -> 4.16 us  [local(): lax.ppermute(own, 'blk', [(i, (i + 1) % tiles) for i in range(tiles)])]
    ppermute x3, starting transfers between devices: 9.98 us -> 11.7 us  [local(): lax.ppermute(x, 'col', [(i, i ^ bit) for i in range(devices)])]
    pallas_call x4, Pallas kernels: 6.11 us -> 7.27 us  [the longest x1 2.25 us: local(): pl.pallas_call(images_kernel, grid=(1,), in_specs=[meta, body, whole(*blo...]
    all_to_all x1, blocking collectives: 23.4 us -> 24.4 us  [local(): parts = lax.all_to_all(parts, 'col', 0, 0, axis_index_groups=groups)]
    ppermute x1, starting transfers between devices: 7.29 us -> 8.12 us  [local(): lax.ppermute(own, 'blk', [((i + 1) % tiles, i) for i in range(tiles)])]
  transfers between devices with their start and end apart: 5 -> 5, of which waited for: 3 -> 2; matrix products, arithmetic and copies ran while one was open for 0% -> 0% of each run, Pallas kernels for 4% -> 4%
where the time goes in v2:
time: 68.1 us; the launch traced here: 67.3 us
  blocking collectives  24.4 us (36%)
  starting transfers between devices  21.8 us (32%)
  waiting for transfers between devices  11.4 us (17%)
  Pallas kernels  8.76 us (13%)
  local copies, waits for them, and re-layouts  0.81 us (1%)
    all_to_all x1, blocking collectives, local(): parts = lax.all_to_all(parts, 'col', 0, 0, axis_index_groups=groups)  24.4 us
    ppermute x3, starting transfers between devices, local(): lax.ppermute(x, 'col', [(i, i ^ bit) for i in range(devices)])  11.7 us
    ppermute x1, starting transfers between devices, local(): lax.ppermute(own, 'blk', [((i + 1) % tiles, i) for i in range(tiles)])  8.12 us
    ppermute x3, waiting for transfers between devices, local(): lax.ppermute(x, 'col', [(i, i ^ bit) for i in range(devices)])  7.19 us
    ppermute x1, waiting for transfers between devices, local(): lax.ppermute(own, 'blk', [(i, (i + 1) % tiles) for i in range(tiles)])  4.16 us
    pallas_call x1, Pallas kernels, local(): pl.pallas_call(images_kernel, grid=(1,), in_specs=[meta, body, whole(*blo...  2.25 us
    pallas_call x1, Pallas kernels, local(): pl.pallas_call(select_kernel, in_specs=[pl.BlockSpec(memory_space=pltpu.H...  2.04 us
    ppermute x1, starting transfers between devices, local(): lax.ppermute(own, 'blk', [(i, (i + 1) % tiles) for i in range(tiles)])  1.92 us
  transfers between devices with their start and end apart: 5, of which 2 were waited for; matrix products, arithmetic and copies ran while one was open for 0% of the time, Pallas kernels for 4%

profile of v2, /device:TPU:1, one launch (start us, length us, event | category | flops | bytes accessed | tf_op | source)
XLA Modules:
  0.0 67.3 jit_solution(10316481398453670273)
XLA Ops:
  0.0 0.0 copy-start.4
  0.0 0.0 copy-start.2
  0.0 0.0 copy-start.1
  0.0 2.0 %select.1 = (f32[512,512]{1,0:T(8,128)S(1)}, f32[8,128]{1,0:T(8,128)S(1)}, s32[16,8,128]{2,1,0:T(8,128)S(1)}) custom-call(s32[1,16]{1,0:T(1,128)} %occ_ref.1, s32[1,16]{1,0:T(1,128)} %offset_ref.1, s32[1,16]{1,0:T(1,128)} %other_ref.1, s32[1,16]{1,0:T(1,128)} %blocks_ref.1, f32[4,128,1024]{2,1,0:T(8,128)} %coef_ref.3), custom_call_target="tpu_custom_call" | custom-call | bytes 3145728 | tf_op jit(solution)/shard_map/select/pallas_call | solution.py:150
  2.1 8.1 %collective-permute-start.4 = (f32[512,512]{1,0:T(8,128)S(1)}, f32[512,512]{1,0:T(8,128)S(1)}, u32[]{:S(2)}, u32[]{:S(2)}) collective-permute-start(f32[512,512]{1,0:T(8,128)S(1)} %get-tuple-element.25.own_ref), channel_id=1, source_target_pairs={{16,0},{32,16},{48,32},{64,48},{80,64},{96,80},{112,96},{128,112},... | collective-permute-start | bytes 3145736 | tf_op jit(solution)/shard_map/ppermute | solution.py:168
  10.2 1.9 %collective-permute-start.3 = (f32[512,512]{1,0:T(8,128)S(1)}, f32[512,512]{1,0:T(8,128)S(1)}, u32[]{:S(2)}, u32[]{:S(2)}) collective-permute-start(f32[512,512]{1,0:T(8,128)S(1)} %get-tuple-element.25.own_ref), channel_id=1, source_target_pairs={{0,16},{16,32},{32,48},{48,64},{64,80},{80,96},{96,112},{112,128},... | collective-permute-start | bytes 3145736 | tf_op jit(solution)/shard_map/ppermute | solution.py:167
  12.1 0.0 copy-done.4
  12.2 0.0 copy-done.2
  12.2 0.0 copy-done.1
  12.2 1.2 %lagrangian.1 = (f32[1032,128]{1,0:T(8,128)S(1)}, f32[1032,128]{1,0:T(8,128)S(1)}) custom-call(f32[8,128]{1,0:T(8,128)S(1)} %get-tuple-element.19.meta_ref, s32[16,8,128]{2,1,0:T(8,128)S(1)} %get-tuple-element.20.kept_ref, f32[1,16,128,128]{3,2,1,0:T(8,128)S(1)} %copy-done.1, f32[1,16,128,128]{3,2,1,0:T(8,128)S(1)} %copy-done.2), custom_call_target="tpu_custom_call" | custom-call | flops 201326592 | bytes 3145728 | tf_op jit(solution)/shard_map/lagrangian/pallas_call | solution.py:171
  13.4 0.0 copy-start.3
  13.4 0.8 %copy-done.3 = f32[1032,128]{1,0:T(8,128)} copy-done((f32[1032,128]{1,0:T(8,128)}, f32[1032,128]{1,0:T(8,128)S(1)}, u32[]{:S(2)}) %copy-start.3) | copy-done | bytes 528408
  14.2 14.3 %conditional.1 = (f32[1032,128]{1,0:T(8,128)}, f32[1032,128]{1,0:T(8,128)}) conditional(s32[]{:T(128)} %bitcast, () %tuple.13, (f32[1032,128]{1,0:T(8,128)S(1)}, f32[1032,128]{1,0:T(8,128)S(1)}) %tuple.14), branch_computations={%region_0.0_spmd, %region_1.0_spmd} | conditional | bytes 4227168 | solution.py:180
  14.2 4.0 %collective-permute-start = (f32[1032,128]{1,0:T(8,128)S(1)}, f32[1032,128]{1,0:T(8,128)}, u32[]{:S(2)}, u32[]{:S(2)}) collective-permute-start(f32[1032,128]{1,0:T(8,128)S(1)} %get-tuple-element.9), channel_id=1, source_target_pairs={{0,2},{1,3},{2,0},{3,1},{4,6},{5,7},{6,4},{7,5},{8,10},{9,11},{10,... | collective-permute-start | bytes 1585160 | tf_op jit(solution)/shard_map/cond/branch_1_fun/ppermute | solution.py:179
  18.2 3.1 %collective-permute-start.1 = (f32[1032,128]{1,0:T(8,128)S(1)}, f32[1032,128]{1,0:T(8,128)}, u32[]{:S(2)}, u32[]{:S(2)}) collective-permute-start(f32[1032,128]{1,0:T(8,128)S(1)} %get-tuple-element.10), channel_id=1, source_target_pairs={{0,1},{1,0},{2,3},{3,2},{4,5},{5,4},{6,7},{7,6},{8,9},{9,8},{10,11... | collective-permute-start | bytes 1585160 | tf_op jit(solution)/shard_map/cond/branch_1_fun/ppermute | solution.py:179
  21.3 7.2 %collective-permute-done = f32[1032,128]{1,0:T(8,128)} collective-permute-done((f32[1032,128]{1,0:T(8,128)S(1)}, f32[1032,128]{1,0:T(8,128)}, u32[]{:S(2)}, u32[]{:S(2)}) %collective-permute-start) | collective-permute-done | bytes 528416 | tf_op jit(solution)/shard_map/cond/branch_1_fun/ppermute | solution.py:179
  28.5 0.0 collective-permute-done.1
  28.5 4.6 %collective-permute-start.2 = (f32[1032,128]{1,0:T(8,128)}, f32[1032,128]{1,0:T(8,128)S(1)}, u32[]{:S(2)}, u32[]{:S(2)}) collective-permute-start(f32[1032,128]{1,0:T(8,128)} %get-tuple-element.23.m2.l2), channel_id=1, source_target_pairs={{0,1},{1,0},{2,3},{3,2},{4,5},{5,4},{6,7},{7,6},{8,9},{9,8},{10,11... | collective-permute-start | bytes 1585160 | tf_op jit(solution)/shard_map/ppermute | solution.py:179
  33.2 1.8 %gather.1.some_ref = f32[48,64,128]{2,1,0:T(8,128)S(1)} custom-call(f32[1032,128]{1,0:T(8,128)} %copy-done.3, f32[1032,128]{1,0:T(8,128)} %get-tuple-element.24.m1.l1, f32[1032,128]{1,0:T(8,128)} %get-tuple-element.23.m2.l2, f32[1032,128]{1,0:T(8,128)} %copy-done.3, f32[1032,128]{1,0:T(8,128)} %get-tuple-element.24.m1.l1, f32[1032,128]{1,0:T(8,128)} %get-tuple-element.23.m2.l2), custom_call_target="tpu_custom_call" | custom-call | tf_op jit(solution)/shard_map/gather/pallas_call | solution.py:191
  34.9 0.0 collective-permute-done.2.meta_ref.lag_ref
  34.9 0.0 collective-permute-done.4.next_ref
  34.9 4.2 %collective-permute-done.3.prev_ref = f32[512,512]{1,0:T(8,128)S(1)} collective-permute-done((f32[512,512]{1,0:T(8,128)S(1)}, f32[512,512]{1,0:T(8,128)S(1)}, u32[]{:S(2)}, u32[]{:S(2)}) %collective-permute-start.3) | collective-permute-done | bytes 1048608 | tf_op jit(solution)/shard_map/ppermute | solution.py:167
  39.1 0.0 copy-start
  39.1 2.3 %images.1 = (f32[8,128,128]{2,1,0:T(8,128)S(1)}, f32[48,64,128]{2,1,0:T(8,128)S(1)}) custom-call(f32[1032,128]{1,0:T(8,128)S(1)} %collective-permute-done.2.meta_ref.lag_ref, f32[1032,128]{1,0:T(8,128)S(1)} %collective-permute-done.2.meta_ref.lag_ref, f32[48,64,128]{2,1,0:T(8,128)S(1)} %gather.1.some_ref, ...), custom_call_target="tpu_custom_call", output_to_operand_aliasing={{1}: (2, {})} | custom-call | flops 1207959552 | bytes 4194304 | tf_op jit(solution)/shard_map/images/pallas_call | solution.py:202
  41.4 24.4 %all_to_all.5.part_ref = f32[8,128,128]{2,1,0:T(8,128)S(1)} all-to-all(f32[8,128,128]{2,1,0:T(8,128)S(1)} %get-tuple-element.26), channel_id=1, replica_groups={{0,2,4,6,8,10,12,14},{1,3,5,7,9,11,13,15},{16,18,20,22,24,26,28,30},{17..., dimensions={0} | all-to-all | bytes 1048576 | tf_op jit(solution)/shard_map/all_to_all | solution.py:217
  65.8 0.0 copy-done
  65.8 1.5 %density.1 = f32[64,1024]{1,0:T(8,128)} custom-call(f32[8,128,128]{2,1,0:T(8,128)S(1)} %all_to_all.5.part_ref, f32[4,128,1024]{2,1,0:T(8,128)S(1)} %copy-done), custom_call_target="tpu_custom_call" | custom-call | flops 201326592 | bytes 3145728 | tf_op jit(solution)/shard_map/density/pallas_call | solution.py:219
Async XLA Ops:
  0.0 12.1 %copy-start.4 = (s32[1,16]{1,0:T(1,128)S(1)}, s32[1,16]{1,0:T(1,128)}, u32[]{:S(2)}) copy-start(s32[1,16]{1,0:T(1,128)} %blocks_ref.1) | copy-start | bytes 196
  0.0 12.2 %copy-start.2 = (f32[1,16,128,128]{3,2,1,0:T(8,128)S(1)}, f32[1,16,128,128]{3,2,1,0:T(8,128)}, u32[]{:S(2)}) copy-start(f32[1,16,128,128]{3,2,1,0:T(8,128)} %int_ref.1) | copy-start | bytes 3145732
  0.0 12.2 %copy-start.1 = (f32[1,16,128,128]{3,2,1,0:T(8,128)S(1)}, f32[1,16,128,128]{3,2,1,0:T(8,128)}, u32[]{:S(2)}) copy-start(f32[1,16,128,128]{3,2,1,0:T(8,128)} %amp_ref.1) | copy-start | bytes 3145732
  2.1 32.9 %collective-permute-start.4 = (f32[512,512]{1,0:T(8,128)S(1)}, f32[512,512]{1,0:T(8,128)S(1)}, u32[]{:S(2)}, u32[]{:S(2)}) collective-permute-start(f32[512,512]{1,0:T(8,128)S(1)} %get-tuple-element.25.own_ref), channel_id=1, source_target_pairs={{16,0},{32,16},{48,32},{64,48},{80,64},{96,80},{112,96},{128,112},... | collective-permute-start | bytes 3145736 | tf_op jit(solution)/shard_map/ppermute | solution.py:168
  10.2 28.9 %collective-permute-start.3 = (f32[512,512]{1,0:T(8,128)S(1)}, f32[512,512]{1,0:T(8,128)S(1)}, u32[]{:S(2)}, u32[]{:S(2)}) collective-permute-start(f32[512,512]{1,0:T(8,128)S(1)} %get-tuple-element.25.own_ref), channel_id=1, source_target_pairs={{0,16},{16,32},{32,48},{48,64},{64,80},{80,96},{96,112},{112,128},... | collective-permute-start | bytes 3145736 | tf_op jit(solution)/shard_map/ppermute | solution.py:167
  13.4 0.8 %copy-start.3 = (f32[1032,128]{1,0:T(8,128)}, f32[1032,128]{1,0:T(8,128)S(1)}, u32[]{:S(2)}) copy-start(f32[1032,128]{1,0:T(8,128)S(1)} %get-tuple-element.22.m0.l0) | copy-start | bytes 1585156
  14.2 14.3 %collective-permute-start = (f32[1032,128]{1,0:T(8,128)S(1)}, f32[1032,128]{1,0:T(8,128)}, u32[]{:S(2)}, u32[]{:S(2)}) collective-permute-start(f32[1032,128]{1,0:T(8,128)S(1)} %get-tuple-element.9), channel_id=1, source_target_pairs={{0,2},{1,3},{2,0},{3,1},{4,6},{5,7},{6,4},{7,5},{8,10},{9,11},{10,... | collective-permute-start | bytes 1585160 | tf_op jit(solution)/shard_map/cond/branch_1_fun/ppermute | solution.py:179
  18.2 10.3 %collective-permute-start.1 = (f32[1032,128]{1,0:T(8,128)S(1)}, f32[1032,128]{1,0:T(8,128)}, u32[]{:S(2)}, u32[]{:S(2)}) collective-permute-start(f32[1032,128]{1,0:T(8,128)S(1)} %get-tuple-element.10), channel_id=1, source_target_pairs={{0,1},{1,0},{2,3},{3,2},{4,5},{5,4},{6,7},{7,6},{8,9},{9,8},{10,11... | collective-permute-start | bytes 1585160 | tf_op jit(solution)/shard_map/cond/branch_1_fun/ppermute | solution.py:179
  28.5 6.4 %collective-permute-start.2 = (f32[1032,128]{1,0:T(8,128)}, f32[1032,128]{1,0:T(8,128)S(1)}, u32[]{:S(2)}, u32[]{:S(2)}) collective-permute-start(f32[1032,128]{1,0:T(8,128)} %get-tuple-element.23.m2.l2), channel_id=1, source_target_pairs={{0,1},{1,0},{2,3},{3,2},{4,5},{5,4},{6,7},{7,6},{8,9},{9,8},{10,11... | collective-permute-start | bytes 1585160 | tf_op jit(solution)/shard_map/ppermute | solution.py:179
  39.1 26.7 %copy-start = (f32[4,128,1024]{2,1,0:T(8,128)S(1)}, f32[4,128,1024]{2,1,0:T(8,128)}, u32[]{:S(2)}) copy-start(f32[4,128,1024]{2,1,0:T(8,128)} %coef_ref.3) | copy-start | bytes 6291460

commit v3 on v2

v3 whole, which is shorter than its diff:
```python
import functools

import jax
import jax.numpy as jnp
from jax import lax
from jax.experimental import pallas as pl
from jax.experimental.pallas import tpu as pltpu
from jax.sharding import PartitionSpec as P

F32 = jnp.float32
BF16 = jnp.bfloat16
ORB = 4
PNO = 128
AO = 1024
SLOTS = 16
CHIPS = 8
WIDE = AO // 2
NARROW = AO // 16
HALF = PNO // 2
ROWS = SLOTS * HALF
META = 8
TILES = 3 * ORB
ARRIVAL = 1 << 33


def split(x):
    hi = x.astype(BF16)
    return hi, (x - hi.astype(F32)).astype(BF16)


def dot(a, b, dims=((1,), (0,))):
    return lax.dot_general(a, b, (dims, ((), ())), preferred_element_type=F32)


def dot3(a, b, dims=((1,), (0,))):
    return dot(a[0], b[0], dims) + (dot(a[0], b[1], dims) + dot(a[1], b[0], dims))


def select_kernel(occ_ref, offset_ref, other_ref, blocks_ref, coef_ref, out_ref, meta_ref, keep_ref, held, numbers, sems):
    copies = [pltpu.make_async_copy(coef_ref.at[o], held.at[o], sems.at[o]) for o in range(ORB)]
    lists = [
        pltpu.make_async_copy(ref, numbers.at[pl.ds(i, 1)], sems.at[ORB + i])
        for i, ref in enumerate((occ_ref, offset_ref, other_ref, blocks_ref))
    ]
    for copy in copies + lists:
        copy.start()
    for copy in lists:
        copy.wait()
    lane = lax.broadcasted_iota(jnp.int32, (META, 128), 1)
    meta = jnp.zeros((META, 128), jnp.int32)
    for p in range(SLOTS):
        block = (numbers[1, p] * ORB + numbers[2, p]) * ORB + numbers[0, p]
        meta = jnp.where(lane == p, block, meta)
        keep_ref[p] = jnp.full((8, 128), PNO // 4 * numbers[3, p], jnp.int32)
    meta_ref[...] = meta.astype(F32)
    left = lax.broadcasted_iota(jnp.int32, (PNO, 128), 1) < NARROW

    def take(core):
        for o, copy in enumerate(copies):
            copy.wait()
            for k in range(CHIPS // 2):
                a = held[o, :, 256 * k : 256 * k + 128]
                b = held[o, :, 256 * k + 128 : 256 * k + 256]
                a, b = (a, pltpu.roll(b, NARROW, 1)) if core == 0 else (pltpu.roll(a, NARROW, 1), b)
                out_ref[o * PNO : (o + 1) * PNO, 128 * k : 128 * k + 128] = jnp.where(left, a, b)

    for core in range(2):
        pl.when(lax.axis_index("col") % 2 == core)(functools.partial(take, core))


def lagrangian_kernel(meta_ref, kept_ref, amp_ref, int_ref, keep_ref, send_ref):
    upper = (lax.axis_index("col") // 2) % 2 == 1
    far = jnp.maximum(
        lax.broadcasted_iota(jnp.int32, (PNO, PNO), 0), lax.broadcasted_iota(jnp.int32, (PNO, PNO), 1)
    )
    for p in range(SLOTS):
        kept = jnp.where(far < kept_ref[p, 0:1, :], amp_ref[0, p], 0.0)
        lag = dot3(split(kept), split(int_ref[0, p]), ((1,), (1,)))
        low, high = lag[:HALF], lag[HALF:]
        at = slice(p * HALF, (p + 1) * HALF)
        keep_ref[at, :] = jnp.where(upper, high, low)
        send_ref[at, :] = jnp.where(upper, low, high)
    keep_ref[ROWS:, :] = meta_ref[...]
    send_ref[ROWS:, :] = meta_ref[...]


def add_slots(block_ref, lag_ref):
    for p in range(SLOTS):
        number = lag_ref[ROWS, p].astype(jnp.int32)
        block_ref[number] += lag_ref[p * HALF : (p + 1) * HALF, :]


def gather_kernel(keep_ref, near_ref, far_ref, block_ref):
    block_ref[...] = jnp.zeros_like(block_ref)
    for lag_ref in (keep_ref, near_ref, far_ref):
        add_slots(block_ref, lag_ref)


def arrived_kernel(second_ref, first_ref, second_out, first_out):
    pass


def images_kernel(lag_ref, some_ref, second_ref, own_ref, first_ref, out_ref, block_ref):
    add_slots(block_ref, lag_ref)
    odd = lax.axis_index("blk") % 2
    total = jnp.zeros((ORB * HALF, WIDE), F32)
    for start, x_ref in ((ORB, own_ref), (2 * ORB * odd, first_ref), (2 * ORB * (1 - odd), second_ref)):
        lhs = jnp.concatenate(
            [
                jnp.concatenate([block_ref[(start + j) * ORB + o] for j in range(ORB)], axis=1)
                for o in range(ORB)
            ],
            axis=0,
        )
        total += dot3(split(lhs), split(x_ref[...]))
    left = lax.broadcasted_iota(jnp.int32, (2 * HALF, 128), 1) < NARROW
    for k in range(CHIPS // 2):
        top = total[: 2 * HALF, 128 * k : 128 * k + 128]
        low = total[2 * HALF :, 128 * k : 128 * k + 128]
        out_ref[2 * k] = jnp.where(left, top, pltpu.roll(low, NARROW, 1))
        out_ref[2 * k + 1] = jnp.where(left, pltpu.roll(top, NARROW, 1), low)


def density_kernel(part_ref, coef_ref, out_ref, held, sems):
    sums = []
    for h in range(2):
        s = (part_ref[h] + part_ref[h + 2]) + (part_ref[h + 4] + part_ref[h + 6])
        sums.append(s.T)
    lhs = jnp.concatenate([s[NARROW * pair : NARROW * (pair + 1)] for pair in range(2) for s in sums], axis=1)
    lhs = jnp.concatenate(split(lhs))
    copies = []
    for n in range(4):
        at = slice(256 * n, 256 * (n + 1))
        rhs = [
            coef_ref[2 * pair + o, HALF * h : HALF * (h + 1), at]
            for pair in range(2)
            for h in range(2)
            for o in range(2)
        ]
        hi, lo = split(jnp.concatenate(rhs, axis=0))
        both = dot(lhs, hi)
        held[:, at] = both[:NARROW] + (both[NARROW:] + dot(lhs[:NARROW], lo))
        copies.append(pltpu.make_async_copy(held.at[:, at], out_ref.at[:, at], sems.at[n]))
        copies[-1].start()
    for copy in copies:
        copy.wait()


def cost(macs, size):
    return pl.CostEstimate(flops=2 * macs, bytes_accessed=size, transcendentals=0)


PARAMS = pltpu.CompilerParams(vmem_limit_bytes=48 * 1024 * 1024)


def local(pair_occ, pair_offset, pair_other, pno_blocks, pno_coef, amplitudes, integrals):
    tiles = lax.axis_size("blk")
    devices = lax.axis_size("col")
    in_place = lambda x: pltpu.with_memory_space_constraint(x, pltpu.HBM)

    own, numbers, kept = pl.pallas_call(
        select_kernel,
        in_specs=[pl.BlockSpec(memory_space=pltpu.HBM)] * 5,
        out_shape=(
            jax.ShapeDtypeStruct((ORB * PNO, WIDE), F32),
            jax.ShapeDtypeStruct((META, 128), F32),
            jax.ShapeDtypeStruct((SLOTS, 8, 128), jnp.int32),
        ),
        scratch_shapes=[
            pltpu.VMEM((ORB, PNO, AO), F32),
            pltpu.SMEM((4, SLOTS), jnp.int32),
            pltpu.SemaphoreType.DMA((ORB + 4,)),
        ],
        compiler_params=PARAMS,
        cost_estimate=cost(0, 3 << 20),
        name="select",
    )(*map(in_place, (pair_occ, pair_offset, pair_other, pno_blocks, pno_coef)))
    second = lax.ppermute(own, "blk", [(i, (i + 1 - 2 * (i % 2)) % tiles) for i in range(tiles)])
    first = lax.ppermute(own, "blk", [(i, (i + 2 * (i % 2) - 1) % tiles) for i in range(tiles)])

    half = jax.ShapeDtypeStruct((ROWS + META, 128), F32)
    keep, send = pl.pallas_call(
        lagrangian_kernel,
        out_shape=(half, half),
        compiler_params=PARAMS,
        cost_estimate=cost(3 * SLOTS * PNO**3, 3 << 20),
        name="lagrangian",
    )(numbers, kept, amplitudes, integrals)

    swap = lambda x, bit: lax.ppermute(x, "col", [(i, i ^ bit) for i in range(devices)])
    far, near = swap(send, 2), swap(keep, 1)
    last = swap(far, 1)

    blocks = jax.ShapeDtypeStruct((TILES * ORB, HALF, PNO), F32)
    some = pl.pallas_call(
        gather_kernel,
        out_shape=blocks,
        compiler_params=PARAMS,
        cost_estimate=cost(0, 0),
        name="gather",
    )(keep, near, far)
    anywhere = [pl.BlockSpec(memory_space=pl.ANY)] * 2
    second, first = pl.pallas_call(
        arrived_kernel,
        in_specs=anywhere,
        out_specs=anywhere,
        out_shape=(jax.ShapeDtypeStruct(own.shape, F32),) * 2,
        input_output_aliases={0: 0, 1: 1},
        compiler_params=PARAMS,
        cost_estimate=cost(ARRIVAL, 0),
        name="arrived",
    )(second, first)
    parts, _ = pl.pallas_call(
        images_kernel,
        out_shape=(jax.ShapeDtypeStruct((CHIPS, 2 * HALF, 128), F32), blocks),
        input_output_aliases={1: 1},
        compiler_params=PARAMS,
        cost_estimate=cost(3 * ORB * HALF * TILES * PNO * WIDE, 4 << 20),
        name="images",
    )(last, some, second, own, first)
    groups = [[2 * z + c for z in range(CHIPS)] for c in range(2)]
    parts = lax.all_to_all(parts, "col", 0, 0, axis_index_groups=groups)

    out = pl.pallas_call(
        density_kernel,
        out_specs=pl.BlockSpec(memory_space=pl.ANY),
        out_shape=jax.ShapeDtypeStruct((NARROW, AO), F32),
        scratch_shapes=[pltpu.VMEM((NARROW, AO), F32), pltpu.SemaphoreType.DMA((4,))],
        compiler_params=PARAMS,
        cost_estimate=cost(3 * ORB * PNO * NARROW * AO, 3 << 20),
        name="density",
    )(parts, pno_coef)
    return out.T[None]


def solution(mesh):
    in_specs = (
        P("blk", "col"),
        P("blk", "col"),
        P("blk", "col"),
        P("blk", "col"),
        P("blk", None, None),
        P("blk", "col", None, None),
        P("blk", "col", None, None),
    )
    out_specs = P("blk", None, "col")
    return jax.shard_map(local, mesh=mesh, in_specs=in_specs, out_specs=out_specs, check_vma=False)
```

time: 68.1 us -> 64.8 us (0.952)
  the two profiles are of different devices: /device:TPU:1 before, /device:TPU:2 now
where the time goes in v3:
time: 64.8 us; the launch traced here: 64.6 us
  blocking collectives  26.7 us (41%)
  starting transfers between devices  18.1 us (28%)
  waiting for transfers between devices  13.1 us (20%)
  Pallas kernels  6.54 us (10%)
    all_to_all x1, blocking collectives, local(): parts = lax.all_to_all(parts, 'col', 0, 0, axis_index_groups=groups)  26.7 us
    ppermute x3, waiting for transfers between devices, local(): lax.ppermute(x, 'col', [(i, i ^ bit) for i in range(devices)])  9.51 us
    ppermute x3, starting transfers between devices, local(): lax.ppermute(x, 'col', [(i, i ^ bit) for i in range(devices)])  8.11 us
    ppermute x1, starting transfers between devices, local(): lax.ppermute(own, 'blk', [(i, (i + 1 - 2 * (i % 2)) % tiles) for i in ran...  6.62 us
    ppermute x1, waiting for transfers between devices, local(): lax.ppermute(own, 'blk', [(i, (i + 1 - 2 * (i % 2)) % tiles) for i in ran...  3.55 us
    ppermute x1, starting transfers between devices, local(): lax.ppermute(own, 'blk', [(i, (i + 2 * (i % 2) - 1) % tiles) for i in ran...  3.4 us
    pallas_call x1, Pallas kernels, local(): pl.pallas_call(select_kernel, in_specs=[pl.BlockSpec(memory_space=pltpu.H...  1.87 us
    pallas_call x1, Pallas kernels, local(): pl.pallas_call(images_kernel, out_shape=(jax.ShapeDtypeStruct((CHIPS, 2 *...  1.79 us
  transfers between devices with their start and end apart: 5, of which 2 were waited for; matrix products, arithmetic and copies ran while one was open for 0% of the time, Pallas kernels for 3%

profile of v3, /device:TPU:2, one launch (start us, length us, event | category | flops | bytes accessed | tf_op | source)
XLA Modules:
  0.0 64.6 jit_solution(9091205189857052972)
XLA Ops:
  0.0 0.0 copy-start.2
  0.0 0.0 copy-start.1
  0.0 1.9 %select.1 = (f32[512,512]{1,0:T(8,128)S(1)}, f32[8,128]{1,0:T(8,128)S(1)}, s32[16,8,128]{2,1,0:T(8,128)S(1)}) custom-call(s32[1,16]{1,0:T(1,128)} %occ_ref.1, s32[1,16]{1,0:T(1,128)} %offset_ref.1, s32[1,16]{1,0:T(1,128)} %other_ref.1, s32[1,16]{1,0:T(1,128)} %blocks_ref.1, f32[4,128,1024]{2,1,0:T(8,128)} %coef_ref.3), custom_call_target="tpu_custom_call" | custom-call | bytes 3145728 | tf_op jit(solution)/shard_map/select/pallas_call | solution.py:161
  1.9 3.4 %collective-permute-start.4 = (f32[512,512]{1,0:T(8,128)S(1)}, f32[512,512]{1,0:T(8,128)S(1)}, u32[]{:S(2)}, u32[]{:S(2)}) collective-permute-start(f32[512,512]{1,0:T(8,128)S(1)} %get-tuple-element.17.own_ref), channel_id=1, source_target_pairs={{0,496},{16,32},{32,16},{48,64},{64,48},{80,96},{96,80},{112,128},... | collective-permute-start | bytes 3145736 | tf_op jit(solution)/shard_map/ppermute | solution.py:179
  5.3 6.6 %collective-permute-start.3 = (f32[512,512]{1,0:T(8,128)S(1)}, f32[512,512]{1,0:T(8,128)S(1)}, u32[]{:S(2)}, u32[]{:S(2)}) collective-permute-start(f32[512,512]{1,0:T(8,128)S(1)} %get-tuple-element.17.own_ref), channel_id=1, source_target_pairs={{0,16},{16,0},{32,48},{48,32},{64,80},{80,64},{96,112},{112,96},{1... | collective-permute-start | bytes 3145736 | tf_op jit(solution)/shard_map/ppermute | solution.py:178
  11.9 0.0 copy-done.2
  11.9 0.0 copy-done.1
  11.9 1.2 %lagrangian.1 = (f32[1032,128]{1,0:T(8,128)S(1)}, f32[1032,128]{1,0:T(8,128)S(1)}) custom-call(f32[8,128]{1,0:T(8,128)S(1)} %get-tuple-element.13.meta_ref, s32[16,8,128]{2,1,0:T(8,128)S(1)} %get-tuple-element.14.kept_ref, f32[1,16,128,128]{3,2,1,0:T(8,128)S(1)} %copy-done.1, f32[1,16,128,128]{3,2,1,0:T(8,128)S(1)} %copy-done.2), custom_call_target="tpu_custom_call" | custom-call | flops 201326592 | bytes 3145728 | tf_op jit(solution)/shard_map/lagrangian/pallas_call | solution.py:182
  13.2 4.3 %collective-permute-start = (f32[1032,128]{1,0:T(8,128)S(1)}, f32[1032,128]{1,0:T(8,128)S(1)}, u32[]{:S(2)}, u32[]{:S(2)}) collective-permute-start(f32[1032,128]{1,0:T(8,128)S(1)} %get-tuple-element.15), channel_id=1, source_target_pairs={{0,2},{1,3},{2,0},{3,1},{4,6},{5,7},{6,4},{7,5},{8,10},{9,11},{10,... | collective-permute-start | bytes 1585160 | tf_op jit(solution)/shard_map/ppermute | solution.py:190
  17.4 1.9 %collective-permute-start.2 = (f32[1032,128]{1,0:T(8,128)S(1)}, f32[1032,128]{1,0:T(8,128)S(1)}, u32[]{:S(2)}, u32[]{:S(2)}) collective-permute-start(f32[1032,128]{1,0:T(8,128)S(1)} %get-tuple-element.16.keep_ref), channel_id=1, source_target_pairs={{0,1},{1,0},{2,3},{3,2},{4,5},{5,4},{6,7},{7,6},{8,9},{9,8},{10,11... | collective-permute-start | bytes 1585160 | tf_op jit(solution)/shard_map/ppermute | solution.py:190
  19.4 9.5 %collective-permute-done.far_ref = f32[1032,128]{1,0:T(8,128)S(1)} collective-permute-done((f32[1032,128]{1,0:T(8,128)S(1)}, f32[1032,128]{1,0:T(8,128)S(1)}, u32[]{:S(2)}, u32[]{:S(2)}) %collective-permute-start) | collective-permute-done | bytes 528416 | tf_op jit(solution)/shard_map/ppermute | solution.py:190
  28.9 1.9 %collective-permute-start.1 = (f32[1032,128]{1,0:T(8,128)S(1)}, f32[1032,128]{1,0:T(8,128)S(1)}, u32[]{:S(2)}, u32[]{:S(2)}) collective-permute-start(f32[1032,128]{1,0:T(8,128)S(1)} %collective-permute-done.far_ref), channel_id=1, source_target_pairs={{0,1},{1,0},{2,3},{3,2},{4,5},{5,4},{6,7},{7,6},{8,9},{9,8},{10,11... | collective-permute-start | bytes 1585160 | tf_op jit(solution)/shard_map/ppermute | solution.py:190
  30.8 0.0 collective-permute-done.2.near_ref
  30.8 0.4 gather.1.some_ref
  31.2 0.0 collective-permute-done.4.first_ref
  31.2 3.5 %collective-permute-done.3.second_ref = f32[512,512]{1,0:T(8,128)S(1)} collective-permute-done((f32[512,512]{1,0:T(8,128)S(1)}, f32[512,512]{1,0:T(8,128)S(1)}, u32[]{:S(2)}, u32[]{:S(2)}) %collective-permute-start.3) | collective-permute-done | bytes 1048608 | tf_op jit(solution)/shard_map/ppermute | solution.py:178
  34.8 0.0 collective-permute-done.1.lag_ref
  34.8 0.0 copy-start
  34.8 1.8 %images.1 = (f32[8,128,128]{2,1,0:T(8,128)S(1)}, f32[48,64,128]{2,1,0:T(8,128)S(1)}) custom-call(f32[1032,128]{1,0:T(8,128)S(1)} %collective-permute-done.1.lag_ref, f32[48,64,128]{2,1,0:T(8,128)S(1)} %gather.1.some_ref, f32[512,512]{1,0:T(8,128)S(1)} %get-tuple-element.18.second_ref, ...), custom_call_target="tpu_custom_call", output_to_operand_aliasing={{1}: (1, {})} | custom-call | flops 1207959552 | bytes 4194304 | tf_op jit(solution)/shard_map/images/pallas_call | solution.py:213
  36.6 26.7 %all_to_all.5.part_ref = f32[8,128,128]{2,1,0:T(8,128)S(1)} all-to-all(f32[8,128,128]{2,1,0:T(8,128)S(1)} %get-tuple-element.20), channel_id=1, replica_groups={{0,2,4,6,8,10,12,14},{1,3,5,7,9,11,13,15},{16,18,20,22,24,26,28,30},{17..., dimensions={0} | all-to-all | bytes 1048576 | tf_op jit(solution)/shard_map/all_to_all | solution.py:222
  63.3 0.0 copy-done
  63.3 1.3 %density.1 = f32[64,1024]{1,0:T(8,128)} custom-call(f32[8,128,128]{2,1,0:T(8,128)S(1)} %all_to_all.5.part_ref, f32[4,128,1024]{2,1,0:T(8,128)S(1)} %copy-done), custom_call_target="tpu_custom_call" | custom-call | flops 201326592 | bytes 3145728 | tf_op jit(solution)/shard_map/density/pallas_call | solution.py:224
  (1 shorter events, 0.0 us)
Async XLA Ops:
  0.0 11.9 %copy-start.2 = (f32[1,16,128,128]{3,2,1,0:T(8,128)S(1)}, f32[1,16,128,128]{3,2,1,0:T(8,128)}, u32[]{:S(2)}) copy-start(f32[1,16,128,128]{3,2,1,0:T(8,128)} %int_ref.1) | copy-start | bytes 3145732
  0.0 11.9 %copy-start.1 = (f32[1,16,128,128]{3,2,1,0:T(8,128)S(1)}, f32[1,16,128,128]{3,2,1,0:T(8,128)}, u32[]{:S(2)}) copy-start(f32[1,16,128,128]{3,2,1,0:T(8,128)} %amp_ref.1) | copy-start | bytes 3145732
  1.9 29.3 %collective-permute-start.4 = (f32[512,512]{1,0:T(8,128)S(1)}, f32[512,512]{1,0:T(8,128)S(1)}, u32[]{:S(2)}, u32[]{:S(2)}) collective-permute-start(f32[512,512]{1,0:T(8,128)S(1)} %get-tuple-element.17.own_ref), channel_id=1, source_target_pairs={{0,496},{16,32},{32,16},{48,64},{64,48},{80,96},{96,80},{112,128},... | collective-permute-start | bytes 3145736 | tf_op jit(solution)/shard_map/ppermute | solution.py:179
  5.3 29.5 %collective-permute-start.3 = (f32[512,512]{1,0:T(8,128)S(1)}, f32[512,512]{1,0:T(8,128)S(1)}, u32[]{:S(2)}, u32[]{:S(2)}) collective-permute-start(f32[512,512]{1,0:T(8,128)S(1)} %get-tuple-element.17.own_ref), channel_id=1, source_target_pairs={{0,16},{16,0},{32,48},{48,32},{64,80},{80,64},{96,112},{112,96},{1... | collective-permute-start | bytes 3145736 | tf_op jit(solution)/shard_map/ppermute | solution.py:178
  13.2 15.7 %collective-permute-start = (f32[1032,128]{1,0:T(8,128)S(1)}, f32[1032,128]{1,0:T(8,128)S(1)}, u32[]{:S(2)}, u32[]{:S(2)}) collective-permute-start(f32[1032,128]{1,0:T(8,128)S(1)} %get-tuple-element.15), channel_id=1, source_target_pairs={{0,2},{1,3},{2,0},{3,1},{4,6},{5,7},{6,4},{7,5},{8,10},{9,11},{10,... | collective-permute-start | bytes 1585160 | tf_op jit(solution)/shard_map/ppermute | solution.py:190
  17.4 13.4 %collective-permute-start.2 = (f32[1032,128]{1,0:T(8,128)S(1)}, f32[1032,128]{1,0:T(8,128)S(1)}, u32[]{:S(2)}, u32[]{:S(2)}) collective-permute-start(f32[1032,128]{1,0:T(8,128)S(1)} %get-tuple-element.16.keep_ref), channel_id=1, source_target_pairs={{0,1},{1,0},{2,3},{3,2},{4,5},{5,4},{6,7},{7,6},{8,9},{9,8},{10,11... | collective-permute-start | bytes 1585160 | tf_op jit(solution)/shard_map/ppermute | solution.py:190
  28.9 5.9 %collective-permute-start.1 = (f32[1032,128]{1,0:T(8,128)S(1)}, f32[1032,128]{1,0:T(8,128)S(1)}, u32[]{:S(2)}, u32[]{:S(2)}) collective-permute-start(f32[1032,128]{1,0:T(8,128)S(1)} %collective-permute-done.far_ref), channel_id=1, source_target_pairs={{0,1},{1,0},{2,3},{3,2},{4,5},{5,4},{6,7},{7,6},{8,9},{9,8},{10,11... | collective-permute-start | bytes 1585160 | tf_op jit(solution)/shard_map/ppermute | solution.py:190
  34.8 28.5 %copy-start = (f32[4,128,1024]{2,1,0:T(8,128)S(1)}, f32[4,128,1024]{2,1,0:T(8,128)}, u32[]{:S(2)}) copy-start(f32[4,128,1024]{2,1,0:T(8,128)} %coef_ref.3) | copy-start | bytes 6291460

commit v4 on v3

--- a/solution.py
+++ b/solution.py
@@ -15,6 +15,7 @@
 SLOTS = 16
 CHIPS = 8
 WIDE = AO // 2
+ORDER = (6, 7, 4, 5, 3, 2, 1, 0)
 NARROW = AO // 16
 HALF = PNO // 2
 ROWS = SLOTS * HALF
@@ -117,15 +118,15 @@
     for k in range(CHIPS // 2):
         top = total[: 2 * HALF, 128 * k : 128 * k + 128]
         low = total[2 * HALF :, 128 * k : 128 * k + 128]
-        out_ref[2 * k] = jnp.where(left, top, pltpu.roll(low, NARROW, 1))
-        out_ref[2 * k + 1] = jnp.where(left, pltpu.roll(top, NARROW, 1), low)
+        out_ref[ORDER.index(2 * k)] = jnp.where(left, top, pltpu.roll(low, NARROW, 1))
+        out_ref[ORDER.index(2 * k + 1)] = jnp.where(left, pltpu.roll(top, NARROW, 1), low)
 
 
 def density_kernel(part_ref, coef_ref, out_ref, held, sems):
     sums = []
     for h in range(2):
-        s = (part_ref[h] + part_ref[h + 2]) + (part_ref[h + 4] + part_ref[h + 6])
-        sums.append(s.T)
+        a, b, c, d = (part_ref[ORDER.index(z)] for z in range(h, CHIPS, 2))
+        sums.append(((a + b) + (c + d)).T)
     lhs = jnp.concatenate([s[NARROW * pair : NARROW * (pair + 1)] for pair in range(2) for s in sums], axis=1)
     lhs = jnp.concatenate(split(lhs))
     copies = []
@@ -218,7 +219,7 @@
         cost_estimate=cost(3 * ORB * HALF * TILES * PNO * WIDE, 4 << 20),
         name="images",
     )(last, some, second, own, first)
-    groups = [[2 * z + c for z in range(CHIPS)] for c in range(2)]
+    groups = [[2 * z + c for z in ORDER] for c in range(2)]
     parts = lax.all_to_all(parts, "col", 0, 0, axis_index_groups=groups)
 
     out = pl.pallas_call(

time: 64.8 us -> 61.6 us (0.951)
  the two profiles are of different devices: /device:TPU:2 before, /device:TPU:64 now
where the time goes in v4:
time: 61.6 us; the launch traced here: 61.4 us
  blocking collectives  22.3 us (36%)
  waiting for transfers between devices  17.2 us (28%)
  starting transfers between devices  15.2 us (25%)
  Pallas kernels  6.54 us (11%)
    all_to_all x1, blocking collectives, local(): parts = lax.all_to_all(parts, 'col', 0, 0, axis_index_groups=groups)  22.3 us
    ppermute x3, waiting for transfers between devices, local(): lax.ppermute(x, 'col', [(i, i ^ bit) for i in range(devices)])  11.5 us
    ppermute x1, starting transfers between devices, local(): lax.ppermute(own, 'blk', [(i, (i + 2 * (i % 2) - 1) % tiles) for i in ran...  7.57 us
    ppermute x3, starting transfers between devices, local(): lax.ppermute(x, 'col', [(i, i ^ bit) for i in range(devices)])  5.75 us
    ppermute x1, waiting for transfers between devices, local(): lax.ppermute(own, 'blk', [(i, (i + 1 - 2 * (i % 2)) % tiles) for i in ran...  3.37 us
    ppermute x1, waiting for transfers between devices, local(): lax.ppermute(own, 'blk', [(i, (i + 2 * (i % 2) - 1) % tiles) for i in ran...  2.27 us
    ppermute x1, starting transfers between devices, local(): lax.ppermute(own, 'blk', [(i, (i + 1 - 2 * (i % 2)) % tiles) for i in ran...  1.92 us
    pallas_call x1, Pallas kernels, local(): pl.pallas_call(select_kernel, in_specs=[pl.BlockSpec(memory_space=pltpu.H...  1.87 us
  transfers between devices with their start and end apart: 5, of which 3 were waited for; matrix products, arithmetic and copies ran while one was open for 0% of the time, Pallas kernels for 3%

profile of v4, /device:TPU:64, one launch (start us, length us, event | category | flops | bytes accessed | tf_op | source)
XLA Modules:
  0.0 61.4 jit_solution(8643254589233740008)
XLA Ops:
  0.0 0.0 copy-start.2
  0.0 0.0 copy-start.1
  0.0 1.9 %select.1 = (f32[512,512]{1,0:T(8,128)S(1)}, f32[8,128]{1,0:T(8,128)S(1)}, s32[16,8,128]{2,1,0:T(8,128)S(1)}) custom-call(s32[1,16]{1,0:T(1,128)} %occ_ref.1, s32[1,16]{1,0:T(1,128)} %offset_ref.1, s32[1,16]{1,0:T(1,128)} %other_ref.1, s32[1,16]{1,0:T(1,128)} %blocks_ref.1, f32[4,128,1024]{2,1,0:T(8,128)} %coef_ref.3), custom_call_target="tpu_custom_call" | custom-call | bytes 3145728 | tf_op jit(solution)/shard_map/select/pallas_call | solution.py:162
  1.9 7.6 %collective-permute-start.4 = (f32[512,512]{1,0:T(8,128)S(1)}, f32[512,512]{1,0:T(8,128)S(1)}, u32[]{:S(2)}, u32[]{:S(2)}) collective-permute-start(f32[512,512]{1,0:T(8,128)S(1)} %get-tuple-element.17.own_ref), channel_id=1, source_target_pairs={{0,496},{16,32},{32,16},{48,64},{64,48},{80,96},{96,80},{112,128},... | collective-permute-start | bytes 3145736 | tf_op jit(solution)/shard_map/ppermute | solution.py:180
  9.5 1.9 %collective-permute-start.3 = (f32[512,512]{1,0:T(8,128)S(1)}, f32[512,512]{1,0:T(8,128)S(1)}, u32[]{:S(2)}, u32[]{:S(2)}) collective-permute-start(f32[512,512]{1,0:T(8,128)S(1)} %get-tuple-element.17.own_ref), channel_id=1, source_target_pairs={{0,16},{16,0},{32,48},{48,32},{64,80},{80,64},{96,112},{112,96},{1... | collective-permute-start | bytes 3145736 | tf_op jit(solution)/shard_map/ppermute | solution.py:179
  11.4 0.0 copy-done.2
  11.4 0.0 copy-done.1
  11.4 1.2 %lagrangian.1 = (f32[1032,128]{1,0:T(8,128)S(1)}, f32[1032,128]{1,0:T(8,128)S(1)}) custom-call(f32[8,128]{1,0:T(8,128)S(1)} %get-tuple-element.13.meta_ref, s32[16,8,128]{2,1,0:T(8,128)S(1)} %get-tuple-element.14.kept_ref, f32[1,16,128,128]{3,2,1,0:T(8,128)S(1)} %copy-done.1, f32[1,16,128,128]{3,2,1,0:T(8,128)S(1)} %copy-done.2), custom_call_target="tpu_custom_call" | custom-call | flops 201326592 | bytes 3145728 | tf_op jit(solution)/shard_map/lagrangian/pallas_call | solution.py:183
  12.6 1.9 %collective-permute-start = (f32[1032,128]{1,0:T(8,128)S(1)}, f32[1032,128]{1,0:T(8,128)S(1)}, u32[]{:S(2)}, u32[]{:S(2)}) collective-permute-start(f32[1032,128]{1,0:T(8,128)S(1)} %get-tuple-element.15), channel_id=1, source_target_pairs={{0,2},{1,3},{2,0},{3,1},{4,6},{5,7},{6,4},{7,5},{8,10},{9,11},{10,... | collective-permute-start | bytes 1585160 | tf_op jit(solution)/shard_map/ppermute | solution.py:191
  14.6 1.9 %collective-permute-start.2 = (f32[1032,128]{1,0:T(8,128)S(1)}, f32[1032,128]{1,0:T(8,128)S(1)}, u32[]{:S(2)}, u32[]{:S(2)}) collective-permute-start(f32[1032,128]{1,0:T(8,128)S(1)} %get-tuple-element.16.keep_ref), channel_id=1, source_target_pairs={{0,1},{1,0},{2,3},{3,2},{4,5},{5,4},{6,7},{7,6},{8,9},{9,8},{10,11... | collective-permute-start | bytes 1585160 | tf_op jit(solution)/shard_map/ppermute | solution.py:191
  16.5 11.5 %collective-permute-done.far_ref = f32[1032,128]{1,0:T(8,128)S(1)} collective-permute-done((f32[1032,128]{1,0:T(8,128)S(1)}, f32[1032,128]{1,0:T(8,128)S(1)}, u32[]{:S(2)}, u32[]{:S(2)}) %collective-permute-start) | collective-permute-done | bytes 528416 | tf_op jit(solution)/shard_map/ppermute | solution.py:191
  28.0 1.9 %collective-permute-start.1 = (f32[1032,128]{1,0:T(8,128)S(1)}, f32[1032,128]{1,0:T(8,128)S(1)}, u32[]{:S(2)}, u32[]{:S(2)}) collective-permute-start(f32[1032,128]{1,0:T(8,128)S(1)} %collective-permute-done.far_ref), channel_id=1, source_target_pairs={{0,1},{1,0},{2,3},{3,2},{4,5},{5,4},{6,7},{7,6},{8,9},{9,8},{10,11... | collective-permute-start | bytes 1585160 | tf_op jit(solution)/shard_map/ppermute | solution.py:191
  29.9 0.0 collective-permute-done.2.near_ref
  29.9 0.4 gather.1.some_ref
  30.3 2.3 %collective-permute-done.4.first_ref = f32[512,512]{1,0:T(8,128)S(1)} collective-permute-done((f32[512,512]{1,0:T(8,128)S(1)}, f32[512,512]{1,0:T(8,128)S(1)}, u32[]{:S(2)}, u32[]{:S(2)}) %collective-permute-start.4) | collective-permute-done | bytes 1048608 | tf_op jit(solution)/shard_map/ppermute | solution.py:180
  32.6 3.4 %collective-permute-done.3.second_ref = f32[512,512]{1,0:T(8,128)S(1)} collective-permute-done((f32[512,512]{1,0:T(8,128)S(1)}, f32[512,512]{1,0:T(8,128)S(1)}, u32[]{:S(2)}, u32[]{:S(2)}) %collective-permute-start.3) | collective-permute-done | bytes 1048608 | tf_op jit(solution)/shard_map/ppermute | solution.py:179
  36.0 0.0 collective-permute-done.1.lag_ref
  36.0 0.0 copy-start
  36.0 1.8 %images.1 = (f32[8,128,128]{2,1,0:T(8,128)S(1)}, f32[48,64,128]{2,1,0:T(8,128)S(1)}) custom-call(f32[1032,128]{1,0:T(8,128)S(1)} %collective-permute-done.1.lag_ref, f32[48,64,128]{2,1,0:T(8,128)S(1)} %gather.1.some_ref, f32[512,512]{1,0:T(8,128)S(1)} %get-tuple-element.18.second_ref, ...), custom_call_target="tpu_custom_call", output_to_operand_aliasing={{1}: (1, {})} | custom-call | flops 1207959552 | bytes 4194304 | tf_op jit(solution)/shard_map/images/pallas_call | solution.py:214
  37.8 22.3 %all_to_all.5.part_ref = f32[8,128,128]{2,1,0:T(8,128)S(1)} all-to-all(f32[8,128,128]{2,1,0:T(8,128)S(1)} %get-tuple-element.20), channel_id=1, replica_groups={{12,14,8,10,6,4,2,0},{13,15,9,11,7,5,3,1},{28,30,24,26,22,20,18,16},{29..., dimensions={0} | all-to-all | bytes 1048576 | tf_op jit(solution)/shard_map/all_to_all | solution.py:223
  60.1 0.0 copy-done
  60.1 1.3 %density.1 = f32[64,1024]{1,0:T(8,128)} custom-call(f32[8,128,128]{2,1,0:T(8,128)S(1)} %all_to_all.5.part_ref, f32[4,128,1024]{2,1,0:T(8,128)S(1)} %copy-done), custom_call_target="tpu_custom_call" | custom-call | flops 201326592 | bytes 3145728 | tf_op jit(solution)/shard_map/density/pallas_call | solution.py:225
  (1 shorter events, 0.0 us)
Async XLA Ops:
  0.0 11.4 %copy-start.2 = (f32[1,16,128,128]{3,2,1,0:T(8,128)S(1)}, f32[1,16,128,128]{3,2,1,0:T(8,128)}, u32[]{:S(2)}) copy-start(f32[1,16,128,128]{3,2,1,0:T(8,128)} %int_ref.1) | copy-start | bytes 3145732
  0.0 11.4 %copy-start.1 = (f32[1,16,128,128]{3,2,1,0:T(8,128)S(1)}, f32[1,16,128,128]{3,2,1,0:T(8,128)}, u32[]{:S(2)}) copy-start(f32[1,16,128,128]{3,2,1,0:T(8,128)} %amp_ref.1) | copy-start | bytes 3145732
  1.9 30.7 %collective-permute-start.4 = (f32[512,512]{1,0:T(8,128)S(1)}, f32[512,512]{1,0:T(8,128)S(1)}, u32[]{:S(2)}, u32[]{:S(2)}) collective-permute-start(f32[512,512]{1,0:T(8,128)S(1)} %get-tuple-element.17.own_ref), channel_id=1, source_target_pairs={{0,496},{16,32},{32,16},{48,64},{64,48},{80,96},{96,80},{112,128},... | collective-permute-start | bytes 3145736 | tf_op jit(solution)/shard_map/ppermute | solution.py:180
  9.5 26.5 %collective-permute-start.3 = (f32[512,512]{1,0:T(8,128)S(1)}, f32[512,512]{1,0:T(8,128)S(1)}, u32[]{:S(2)}, u32[]{:S(2)}) collective-permute-start(f32[512,512]{1,0:T(8,128)S(1)} %get-tuple-element.17.own_ref), channel_id=1, source_target_pairs={{0,16},{16,0},{32,48},{48,32},{64,80},{80,64},{96,112},{112,96},{1... | collective-permute-start | bytes 3145736 | tf_op jit(solution)/shard_map/ppermute | solution.py:179
  12.6 15.4 %collective-permute-start = (f32[1032,128]{1,0:T(8,128)S(1)}, f32[1032,128]{1,0:T(8,128)S(1)}, u32[]{:S(2)}, u32[]{:S(2)}) collective-permute-start(f32[1032,128]{1,0:T(8,128)S(1)} %get-tuple-element.15), channel_id=1, source_target_pairs={{0,2},{1,3},{2,0},{3,1},{4,6},{5,7},{6,4},{7,5},{8,10},{9,11},{10,... | collective-permute-start | bytes 1585160 | tf_op jit(solution)/shard_map/ppermute | solution.py:191
  14.6 15.4 %collective-permute-start.2 = (f32[1032,128]{1,0:T(8,128)S(1)}, f32[1032,128]{1,0:T(8,128)S(1)}, u32[]{:S(2)}, u32[]{:S(2)}) collective-permute-start(f32[1032,128]{1,0:T(8,128)S(1)} %get-tuple-element.16.keep_ref), channel_id=1, source_target_pairs={{0,1},{1,0},{2,3},{3,2},{4,5},{5,4},{6,7},{7,6},{8,9},{9,8},{10,11... | collective-permute-start | bytes 1585160 | tf_op jit(solution)/shard_map/ppermute | solution.py:191
  28.0 8.0 %collective-permute-start.1 = (f32[1032,128]{1,0:T(8,128)S(1)}, f32[1032,128]{1,0:T(8,128)S(1)}, u32[]{:S(2)}, u32[]{:S(2)}) collective-permute-start(f32[1032,128]{1,0:T(8,128)S(1)} %collective-permute-done.far_ref), channel_id=1, source_target_pairs={{0,1},{1,0},{2,3},{3,2},{4,5},{5,4},{6,7},{7,6},{8,9},{9,8},{10,11... | collective-permute-start | bytes 1585160 | tf_op jit(solution)/shard_map/ppermute | solution.py:191
  36.0 24.1 %copy-start = (f32[4,128,1024]{2,1,0:T(8,128)S(1)}, f32[4,128,1024]{2,1,0:T(8,128)}, u32[]{:S(2)}) copy-start(f32[4,128,1024]{2,1,0:T(8,128)} %coef_ref.3) | copy-start | bytes 6291460

commit v5 on v4

--- a/solution.py
+++ b/solution.py
@@ -17,8 +17,9 @@
 WIDE = AO // 2
 ORDER = (6, 7, 4, 5, 3, 2, 1, 0)
 NARROW = AO // 16
-HALF = PNO // 2
-ROWS = SLOTS * HALF
+PART = 16
+HELD = 3 * PART
+FEWER = 2 * PART
 META = 8
 TILES = 3 * ORB
 ARRIVAL = 1 << 33
@@ -69,73 +70,79 @@
         pl.when(lax.axis_index("col") % 2 == core)(functools.partial(take, core))
 
 
-def lagrangian_kernel(meta_ref, kept_ref, amp_ref, int_ref, keep_ref, send_ref):
-    upper = (lax.axis_index("col") // 2) % 2 == 1
+def lagrangian_kernel(meta_ref, kept_ref, amp_ref, int_ref, keep_ref, up_ref, down_ref, held):
     far = jnp.maximum(
         lax.broadcasted_iota(jnp.int32, (PNO, PNO), 0), lax.broadcasted_iota(jnp.int32, (PNO, PNO), 1)
     )
     for p in range(SLOTS):
         kept = jnp.where(far < kept_ref[p, 0:1, :], amp_ref[0, p], 0.0)
-        lag = dot3(split(kept), split(int_ref[0, p]), ((1,), (1,)))
-        low, high = lag[:HALF], lag[HALF:]
-        at = slice(p * HALF, (p + 1) * HALF)
-        keep_ref[at, :] = jnp.where(upper, high, low)
-        send_ref[at, :] = jnp.where(upper, low, high)
-    keep_ref[ROWS:, :] = meta_ref[...]
-    send_ref[ROWS:, :] = meta_ref[...]
-
-
-def add_slots(block_ref, lag_ref):
-    for p in range(SLOTS):
-        number = lag_ref[ROWS, p].astype(jnp.int32)
-        block_ref[number] += lag_ref[p * HALF : (p + 1) * HALF, :]
-
-
-def gather_kernel(keep_ref, near_ref, far_ref, block_ref):
+        held[p] = dot3(split(kept), split(int_ref[0, p]), ((1,), (1,)))
+    chip = lax.axis_index("col") // 2
+    for ref, step, size in ((keep_ref, 0, HELD), (up_ref, 1, HELD), (down_ref, -1, FEWER)):
+        for t in range(size // PART):
+            start = pl.multiple_of((chip + step - 3 * t + CHIPS) % CHIPS * PART, PART)
+            for p in range(SLOTS):
+                at = p * size + t * PART
+                ref[at : at + PART, :] = held[p, pl.ds(start, PART), :]
+        ref[SLOTS * size :, :] = meta_ref[...]
+
+
+def gather_kernel(keep_ref, below_ref, above_ref, block_ref):
     block_ref[...] = jnp.zeros_like(block_ref)
-    for lag_ref in (keep_ref, near_ref, far_ref):
-        add_slots(block_ref, lag_ref)
+    for lag_ref, size in ((keep_ref, HELD), (below_ref, HELD), (above_ref, FEWER)):
+        for p in range(SLOTS):
+            number = lag_ref[SLOTS * size, p].astype(jnp.int32)
+            block_ref[number, :size, :] += lag_ref[p * size : (p + 1) * size, :]
 
 
 def arrived_kernel(second_ref, first_ref, second_out, first_out):
     pass
 
 
-def images_kernel(lag_ref, some_ref, second_ref, own_ref, first_ref, out_ref, block_ref):
-    add_slots(block_ref, lag_ref)
-    odd = lax.axis_index("blk") % 2
-    total = jnp.zeros((ORB * HALF, WIDE), F32)
+def images_kernel(mine_ref, other_ref, second_ref, own_ref, first_ref, out_ref):
+    odd = (lax.axis_index("blk") + lax.axis_index("col")) % 2
+    size = ORB * HELD
+    total = jnp.zeros((size, WIDE), F32)
     for start, x_ref in ((ORB, own_ref), (2 * ORB * odd, first_ref), (2 * ORB * (1 - odd), second_ref)):
         lhs = jnp.concatenate(
             [
-                jnp.concatenate([block_ref[(start + j) * ORB + o] for j in range(ORB)], axis=1)
+                jnp.concatenate(
+                    [mine_ref[(start + j) * ORB + o] + other_ref[(start + j) * ORB + o] for j in range(ORB)], axis=1
+                )
                 for o in range(ORB)
             ],
             axis=0,
         )
-        total += dot3(split(lhs), split(x_ref[...]))
-    left = lax.broadcasted_iota(jnp.int32, (2 * HALF, 128), 1) < NARROW
+        hi, lo = split(lhs)
+        x_hi, x_lo = split(x_ref[...])
+        both = dot(jnp.concatenate([hi, lo]), x_hi)
+        total += both[:size] + (both[size:] + dot(hi, x_lo))
+    left = lax.broadcasted_iota(jnp.int32, (size // 2, 128), 1) < NARROW
     for k in range(CHIPS // 2):
-        top = total[: 2 * HALF, 128 * k : 128 * k + 128]
-        low = total[2 * HALF :, 128 * k : 128 * k + 128]
+        top = total[: size // 2, 128 * k : 128 * k + 128]
+        low = total[size // 2 :, 128 * k : 128 * k + 128]
         out_ref[ORDER.index(2 * k)] = jnp.where(left, top, pltpu.roll(low, NARROW, 1))
         out_ref[ORDER.index(2 * k + 1)] = jnp.where(left, pltpu.roll(top, NARROW, 1), low)
 
 
 def density_kernel(part_ref, coef_ref, out_ref, held, sems):
     sums = []
-    for h in range(2):
-        a, b, c, d = (part_ref[ORDER.index(z)] for z in range(h, CHIPS, 2))
-        sums.append(((a + b) + (c + d)).T)
-    lhs = jnp.concatenate([s[NARROW * pair : NARROW * (pair + 1)] for pair in range(2) for s in sums], axis=1)
-    lhs = jnp.concatenate(split(lhs))
+    for r in range(CHIPS):
+        for o in range(2):
+            a, b, c = (
+                part_ref[ORDER.index((r + 3 * t) % CHIPS), o * HELD + t * PART : o * HELD + (t + 1) * PART, :]
+                for t in range(3)
+            )
+            sums.append(a + b + c)
+    sums = jnp.concatenate(sums, axis=0).T
+    lhs = jnp.concatenate(split(jnp.concatenate([sums[:NARROW], sums[NARROW:]], axis=1)))
     copies = []
     for n in range(4):
         at = slice(256 * n, 256 * (n + 1))
         rhs = [
-            coef_ref[2 * pair + o, HALF * h : HALF * (h + 1), at]
+            coef_ref[2 * pair + o, r * PART : (r + 1) * PART, at]
             for pair in range(2)
-            for h in range(2)
+            for r in range(CHIPS)
             for o in range(2)
         ]
         hi, lo = split(jnp.concatenate(rhs, axis=0))
@@ -176,30 +183,36 @@
         cost_estimate=cost(0, 3 << 20),
         name="select",
     )(*map(in_place, (pair_occ, pair_offset, pair_other, pno_blocks, pno_coef)))
-    second = lax.ppermute(own, "blk", [(i, (i + 1 - 2 * (i % 2)) % tiles) for i in range(tiles)])
-    first = lax.ppermute(own, "blk", [(i, (i + 2 * (i % 2) - 1) % tiles) for i in range(tiles)])
-
-    half = jax.ShapeDtypeStruct((ROWS + META, 128), F32)
-    keep, send = pl.pallas_call(
+    def halo(turn):
+        pairs = []
+        for b in range(tiles):
+            for q in range(devices):
+                there = (b + 2 * ((b + q + turn) % 2) - 1) % tiles
+                pairs.append((b * devices + q, there * devices + q))
+        return lax.ppermute(own, ("blk", "col"), pairs)
+
+    second, first = halo(1), halo(0)
+
+    pieces = lambda size: jax.ShapeDtypeStruct((SLOTS * size + META, 128), F32)
+    keep, up, down = pl.pallas_call(
         lagrangian_kernel,
-        out_shape=(half, half),
+        out_shape=(pieces(HELD), pieces(HELD), pieces(FEWER)),
+        scratch_shapes=[pltpu.VMEM((SLOTS, PNO, PNO), F32)],
         compiler_params=PARAMS,
         cost_estimate=cost(3 * SLOTS * PNO**3, 3 << 20),
         name="lagrangian",
     )(numbers, kept, amplitudes, integrals)
 
-    swap = lambda x, bit: lax.ppermute(x, "col", [(i, i ^ bit) for i in range(devices)])
-    far, near = swap(send, 2), swap(keep, 1)
-    last = swap(far, 1)
-
-    blocks = jax.ShapeDtypeStruct((TILES * ORB, HALF, PNO), F32)
-    some = pl.pallas_call(
+    shift = lambda x, chips: lax.ppermute(x, "col", [(i, (i + 2 * chips) % devices) for i in range(devices)])
+    mine = pl.pallas_call(
         gather_kernel,
-        out_shape=blocks,
+        out_shape=jax.ShapeDtypeStruct((TILES * ORB, HELD, PNO), F32),
         compiler_params=PARAMS,
         cost_estimate=cost(0, 0),
         name="gather",
-    )(keep, near, far)
+    )(keep, shift(up, 1), shift(down, -1))
+    other = lax.ppermute(mine, "col", [(i, i ^ 1) for i in range(devices)])
+
     anywhere = [pl.BlockSpec(memory_space=pl.ANY)] * 2
     second, first = pl.pallas_call(
         arrived_kernel,
@@ -211,14 +224,13 @@
         cost_estimate=cost(ARRIVAL, 0),
         name="arrived",
     )(second, first)
-    parts, _ = pl.pallas_call(
+    parts = pl.pallas_call(
         images_kernel,
-        out_shape=(jax.ShapeDtypeStruct((CHIPS, 2 * HALF, 128), F32), blocks),
-        input_output_aliases={1: 1},
-        compiler_params=PARAMS,
-        cost_estimate=cost(3 * ORB * HALF * TILES * PNO * WIDE, 4 << 20),
+        out_shape=jax.ShapeDtypeStruct((CHIPS, ORB * HELD // 2, 128), F32),
+        compiler_params=PARAMS,
+        cost_estimate=cost(3 * ORB * HELD * TILES * PNO * WIDE, 4 << 20),
         name="images",
-    )(last, some, second, own, first)
+    )(mine, other, second, own, first)
     groups = [[2 * z + c for z in ORDER] for c in range(2)]
     parts = lax.all_to_all(parts, "col", 0, 0, axis_index_groups=groups)
 

time: 61.6 us -> 57.6 us (0.935)
  the two profiles are of different devices: /device:TPU:64 before, /device:TPU:1 now
where the time goes in v5:
time: 57.6 us; the launch traced here: 57.4 us
  starting transfers between devices  26 us (45%)
  blocking collectives  15.6 us (27%)
  waiting for transfers between devices  9.7 us (17%)
  Pallas kernels  5.96 us (10%)
    all_to_all x1, blocking collectives, local(): parts = lax.all_to_all(parts, 'col', 0, 0, axis_index_groups=groups)  15.6 us
    ppermute x2, starting transfers between devices, local(): lax.ppermute(x, 'col', [(i, (i + 2 * chips) % devices) for i in range(dev...  12.6 us
    ppermute x2, starting transfers between devices, halo(): return lax.ppermute(own, ('blk', 'col'), pairs)  10.6 us
    ppermute x2, waiting for transfers between devices, local(): lax.ppermute(x, 'col', [(i, (i + 2 * chips) % devices) for i in range(dev...  7.27 us
    ppermute x1, starting transfers between devices, local(): other = lax.ppermute(mine, 'col', [(i, i ^ 1) for i in range(devices)])  2.85 us
    ppermute x1, waiting for transfers between devices, local(): other = lax.ppermute(mine, 'col', [(i, i ^ 1) for i in range(devices)])  2.42 us
    pallas_call x1, Pallas kernels, local(): pl.pallas_call(select_kernel, in_specs=[pl.BlockSpec(memory_space=pltpu.H...  1.87 us
    pallas_call x1, Pallas kernels, local(): pl.pallas_call(lagrangian_kernel, out_shape=(pieces(HELD), pieces(HELD),...  1.28 us
  transfers between devices with their start and end apart: 5, of which 3 were waited for; matrix products, arithmetic and copies ran while one was open for 0% of the time, Pallas kernels for 3%

profile of v5, /device:TPU:1, one launch (start us, length us, event | category | flops | bytes accessed | tf_op | source)
XLA Modules:
  0.0 57.4 jit_solution(6437116068078539097)
XLA Ops:
  0.0 0.0 copy-start.2
  0.0 0.0 copy-start.1
  0.0 1.9 %select.1 = (f32[512,512]{1,0:T(8,128)S(1)}, f32[8,128]{1,0:T(8,128)S(1)}, s32[16,8,128]{2,1,0:T(8,128)S(1)}) custom-call(s32[1,16]{1,0:T(1,128)} %occ_ref.1, s32[1,16]{1,0:T(1,128)} %offset_ref.1, s32[1,16]{1,0:T(1,128)} %other_ref.1, s32[1,16]{1,0:T(1,128)} %blocks_ref.1, f32[4,128,1024]{2,1,0:T(8,128)} %coef_ref.3), custom_call_target="tpu_custom_call" | custom-call | bytes 3145728 | tf_op jit(solution)/shard_map/select/pallas_call | solution.py:169
  1.9 3.9 %collective-permute-start.4 = (f32[512,512]{1,0:T(8,128)S(1)}, f32[512,512]{1,0:T(8,128)S(1)}, u32[]{:S(2)}, u32[]{:S(2)}) collective-permute-start(f32[512,512]{1,0:T(8,128)S(1)} %get-tuple-element.18.own_ref), channel_id=1, source_target_pairs={{0,496},{1,17},{2,498},{3,19},{4,500},{5,21},{6,502},{7,23},{8,504... | collective-permute-start | bytes 3145736 | tf_op jit(solution)/shard_map/ppermute | solution.py:192
  5.8 6.6 %collective-permute-start.3 = (f32[512,512]{1,0:T(8,128)S(1)}, f32[512,512]{1,0:T(8,128)S(1)}, u32[]{:S(2)}, u32[]{:S(2)}) collective-permute-start(f32[512,512]{1,0:T(8,128)S(1)} %get-tuple-element.18.own_ref), channel_id=1, source_target_pairs={{0,16},{1,497},{2,18},{3,499},{4,20},{5,501},{6,22},{7,503},{8,24}... | collective-permute-start | bytes 3145736 | tf_op jit(solution)/shard_map/ppermute | solution.py:192
  12.5 0.0 copy-done.2
  12.5 0.0 copy-done.1
  12.5 1.3 %lagrangian.1 = (f32[776,128]{1,0:T(8,128)S(1)}, f32[776,128]{1,0:T(8,128)S(1)}, f32[520,128]{1,0:T(8,128)S(1)}) custom-call(f32[8,128]{1,0:T(8,128)S(1)} %get-tuple-element.13.meta_ref, s32[16,8,128]{2,1,0:T(8,128)S(1)} %get-tuple-element.14.kept_ref, f32[1,16,128,128]{3,2,1,0:T(8,128)S(1)} %copy-done.1, f32[1,16,128,128]{3,2,1,0:T(8,128)S(1)} %copy-done.2), custom_call_target="tpu_custom_call" | custom-call | flops 201326592 | bytes 3145728 | tf_op jit(solution)/shard_map/lagrangian/pallas_call | solution.py:197
  13.8 4.0 %collective-permute-start = (f32[776,128]{1,0:T(8,128)S(1)}, f32[776,128]{1,0:T(8,128)S(1)}, u32[]{:S(2)}, u32[]{:S(2)}) collective-permute-start(f32[776,128]{1,0:T(8,128)S(1)} %get-tuple-element.16), channel_id=1, source_target_pairs={{0,2},{1,3},{2,4},{3,5},{4,6},{5,7},{6,8},{7,9},{8,10},{9,11},{10,... | collective-permute-start | bytes 1191944 | tf_op jit(solution)/shard_map/ppermute | solution.py:206
  17.8 8.6 %collective-permute-start.1 = (f32[520,128]{1,0:T(8,128)S(1)}, f32[520,128]{1,0:T(8,128)S(1)}, u32[]{:S(2)}, u32[]{:S(2)}) collective-permute-start(f32[520,128]{1,0:T(8,128)S(1)} %get-tuple-element.17), channel_id=1, source_target_pairs={{0,14},{1,15},{2,0},{3,1},{4,2},{5,3},{6,4},{7,5},{8,6},{9,7},{10,... | collective-permute-start | bytes 798728 | tf_op jit(solution)/shard_map/ppermute | solution.py:206
  26.4 5.3 %collective-permute-done.1.above_ref = f32[520,128]{1,0:T(8,128)S(1)} collective-permute-done((f32[520,128]{1,0:T(8,128)S(1)}, f32[520,128]{1,0:T(8,128)S(1)}, u32[]{:S(2)}, u32[]{:S(2)}) %collective-permute-start.1) | collective-permute-done | bytes 266272 | tf_op jit(solution)/shard_map/ppermute | solution.py:206
  31.7 1.9 %collective-permute-done.below_ref = f32[776,128]{1,0:T(8,128)S(1)} collective-permute-done((f32[776,128]{1,0:T(8,128)S(1)}, f32[776,128]{1,0:T(8,128)S(1)}, u32[]{:S(2)}, u32[]{:S(2)}) %collective-permute-start) | collective-permute-done | bytes 397344 | tf_op jit(solution)/shard_map/ppermute | solution.py:206
  33.7 0.4 gather.1.mine_ref
  34.0 2.8 %collective-permute-start.2 = (f32[48,48,128]{2,1,0:T(8,128)S(1)}, f32[48,48,128]{2,1,0:T(8,128)S(1)}, u32[]{:S(2)}, u32[]{:S(2)}) collective-permute-start(f32[48,48,128]{2,1,0:T(8,128)S(1)} %gather.1.mine_ref), channel_id=1, source_target_pairs={{0,1},{1,0},{2,3},{3,2},{4,5},{5,4},{6,7},{7,6},{8,9},{9,8},{10,11... | collective-permute-start | bytes 3538952 | tf_op jit(solution)/shard_map/ppermute | solution.py:214
  36.9 0.0 collective-permute-done.4.first_ref
  36.9 0.0 collective-permute-done.3.second_ref
  36.9 2.4 %collective-permute-done.2.other_ref = f32[48,48,128]{2,1,0:T(8,128)S(1)} collective-permute-done((f32[48,48,128]{2,1,0:T(8,128)S(1)}, f32[48,48,128]{2,1,0:T(8,128)S(1)}, u32[]{:S(2)}, u32[]{:S(2)}) %collective-permute-start.2) | collective-permute-done | bytes 1179680 | tf_op jit(solution)/shard_map/ppermute | solution.py:214
  39.4 0.0 copy-start
  39.4 1.2 %images.1 = f32[8,96,128]{2,1,0:T(8,128)S(1)} custom-call(f32[48,48,128]{2,1,0:T(8,128)S(1)} %gather.1.mine_ref, f32[48,48,128]{2,1,0:T(8,128)S(1)} %collective-permute-done.2.other_ref, f32[512,512]{1,0:T(8,128)S(1)} %get-tuple-element.19.second_ref, f32[512,512]{1,0:T(8,128)S(1)} %get-tuple-element.18.own_ref, f32[512,512]{1,0:T(8,128)S(1)} %get-tuple-element.20.first_ref), custom_call_target="tpu_custom_call" | custom-call | flops 905969664 | bytes 4194304 | tf_op jit(solution)/shard_map/images/pallas_call | solution.py:227
  40.6 15.6 %all_to_all.5.part_ref = f32[8,96,128]{2,1,0:T(8,128)S(1)} all-to-all(f32[8,96,128]{2,1,0:T(8,128)S(1)} %images.1), channel_id=1, replica_groups={{12,14,8,10,6,4,2,0},{13,15,9,11,7,5,3,1},{28,30,24,26,22,20,18,16},{29..., dimensions={0} | all-to-all | bytes 786432 | tf_op jit(solution)/shard_map/all_to_all | solution.py:235
  56.1 0.0 copy-done
  56.1 1.2 %density.1 = f32[64,1024]{1,0:T(8,128)} custom-call(f32[8,96,128]{2,1,0:T(8,128)S(1)} %all_to_all.5.part_ref, f32[4,128,1024]{2,1,0:T(8,128)S(1)} %copy-done), custom_call_target="tpu_custom_call" | custom-call | flops 201326592 | bytes 3145728 | tf_op jit(solution)/shard_map/density/pallas_call | solution.py:237
  (1 shorter events, 0.0 us)
Async XLA Ops:
  0.0 12.5 %copy-start.2 = (f32[1,16,128,128]{3,2,1,0:T(8,128)S(1)}, f32[1,16,128,128]{3,2,1,0:T(8,128)}, u32[]{:S(2)}) copy-start(f32[1,16,128,128]{3,2,1,0:T(8,128)} %int_ref.1) | copy-start | bytes 3145732
  0.0 12.5 %copy-start.1 = (f32[1,16,128,128]{3,2,1,0:T(8,128)S(1)}, f32[1,16,128,128]{3,2,1,0:T(8,128)}, u32[]{:S(2)}) copy-start(f32[1,16,128,128]{3,2,1,0:T(8,128)} %amp_ref.1) | copy-start | bytes 3145732
  1.9 35.0 %collective-permute-start.4 = (f32[512,512]{1,0:T(8,128)S(1)}, f32[512,512]{1,0:T(8,128)S(1)}, u32[]{:S(2)}, u32[]{:S(2)}) collective-permute-start(f32[512,512]{1,0:T(8,128)S(1)} %get-tuple-element.18.own_ref), channel_id=1, source_target_pairs={{0,496},{1,17},{2,498},{3,19},{4,500},{5,21},{6,502},{7,23},{8,504... | collective-permute-start | bytes 3145736 | tf_op jit(solution)/shard_map/ppermute | solution.py:192
  5.8 31.1 %collective-permute-start.3 = (f32[512,512]{1,0:T(8,128)S(1)}, f32[512,512]{1,0:T(8,128)S(1)}, u32[]{:S(2)}, u32[]{:S(2)}) collective-permute-start(f32[512,512]{1,0:T(8,128)S(1)} %get-tuple-element.18.own_ref), channel_id=1, source_target_pairs={{0,16},{1,497},{2,18},{3,499},{4,20},{5,501},{6,22},{7,503},{8,24}... | collective-permute-start | bytes 3145736 | tf_op jit(solution)/shard_map/ppermute | solution.py:192
  13.8 19.9 %collective-permute-start = (f32[776,128]{1,0:T(8,128)S(1)}, f32[776,128]{1,0:T(8,128)S(1)}, u32[]{:S(2)}, u32[]{:S(2)}) collective-permute-start(f32[776,128]{1,0:T(8,128)S(1)} %get-tuple-element.16), channel_id=1, source_target_pairs={{0,2},{1,3},{2,4},{3,5},{4,6},{5,7},{6,8},{7,9},{8,10},{9,11},{10,... | collective-permute-start | bytes 1191944 | tf_op jit(solution)/shard_map/ppermute | solution.py:206
  17.8 13.9 %collective-permute-start.1 = (f32[520,128]{1,0:T(8,128)S(1)}, f32[520,128]{1,0:T(8,128)S(1)}, u32[]{:S(2)}, u32[]{:S(2)}) collective-permute-start(f32[520,128]{1,0:T(8,128)S(1)} %get-tuple-element.17), channel_id=1, source_target_pairs={{0,14},{1,15},{2,0},{3,1},{4,2},{5,3},{6,4},{7,5},{8,6},{9,7},{10,... | collective-permute-start | bytes 798728 | tf_op jit(solution)/shard_map/ppermute | solution.py:206
  34.0 5.3 %collective-permute-start.2 = (f32[48,48,128]{2,1,0:T(8,128)S(1)}, f32[48,48,128]{2,1,0:T(8,128)S(1)}, u32[]{:S(2)}, u32[]{:S(2)}) collective-permute-start(f32[48,48,128]{2,1,0:T(8,128)S(1)} %gather.1.mine_ref), channel_id=1, source_target_pairs={{0,1},{1,0},{2,3},{3,2},{4,5},{5,4},{6,7},{7,6},{8,9},{9,8},{10,11... | collective-permute-start | bytes 3538952 | tf_op jit(solution)/shard_map/ppermute | solution.py:214
  39.4 16.8 %copy-start = (f32[4,128,1024]{2,1,0:T(8,128)S(1)}, f32[4,128,1024]{2,1,0:T(8,128)}, u32[]{:S(2)}) copy-start(f32[4,128,1024]{2,1,0:T(8,128)} %coef_ref.3) | copy-start | bytes 6291460

commit v6 on v5

--- a/solution.py
+++ b/solution.py
@@ -100,7 +100,7 @@
 
 
 def images_kernel(mine_ref, other_ref, second_ref, own_ref, first_ref, out_ref):
-    odd = (lax.axis_index("blk") + lax.axis_index("col")) % 2
+    odd = (lax.axis_index("blk") + lax.axis_index("col") + 1) % 2
     size = ORB * HELD
     total = jnp.zeros((size, WIDE), F32)
     for start, x_ref in ((ORB, own_ref), (2 * ORB * odd, first_ref), (2 * ORB * (1 - odd), second_ref)):
@@ -191,7 +191,7 @@
                 pairs.append((b * devices + q, there * devices + q))
         return lax.ppermute(own, ("blk", "col"), pairs)
 
-    second, first = halo(1), halo(0)
+    second, first = halo(0), halo(1)
 
     pieces = lambda size: jax.ShapeDtypeStruct((SLOTS * size + META, 128), F32)
     keep, up, down = pl.pallas_call(

time: 57.6 us -> 56.7 us (0.984)
  waiting for transfers between devices: 9.7 us -> 8.24 us
  starting transfers between devices: 26 us -> 27 us
    ppermute x1, starting transfers between devices: 2.85 us -> 4.31 us  [local(): other = lax.ppermute(mine, 'col', [(i, i ^ 1) for i in range(devices)])]
    ppermute x2, waiting for transfers between devices: 7.27 us -> 5.81 us  [local(): lax.ppermute(x, 'col', [(i, (i + 2 * chips) % devices) for i in range(dev...]
where the time goes in v6:
time: 56.7 us; the launch traced here: 56.4 us
  starting transfers between devices  27 us (48%)
  blocking collectives  15.1 us (27%)
  waiting for transfers between devices  8.24 us (15%)
  Pallas kernels  5.96 us (11%)
    all_to_all x1, blocking collectives, local(): parts = lax.all_to_all(parts, 'col', 0, 0, axis_index_groups=groups)  15.1 us
    ppermute x2, starting transfers between devices, local(): lax.ppermute(x, 'col', [(i, (i + 2 * chips) % devices) for i in range(dev...  12.6 us
    ppermute x2, starting transfers between devices, halo(): return lax.ppermute(own, ('blk', 'col'), pairs)  10 us
    ppermute x2, waiting for transfers between devices, local(): lax.ppermute(x, 'col', [(i, (i + 2 * chips) % devices) for i in range(dev...  5.81 us
    ppermute x1, starting transfers between devices, local(): other = lax.ppermute(mine, 'col', [(i, i ^ 1) for i in range(devices)])  4.31 us
    ppermute x1, waiting for transfers between devices, local(): other = lax.ppermute(mine, 'col', [(i, i ^ 1) for i in range(devices)])  2.42 us
    pallas_call x1, Pallas kernels, local(): pl.pallas_call(select_kernel, in_specs=[pl.BlockSpec(memory_space=pltpu.H...  1.87 us
    pallas_call x1, Pallas kernels, local(): pl.pallas_call(lagrangian_kernel, out_shape=(pieces(HELD), pieces(HELD),...  1.29 us
  transfers between devices with their start and end apart: 5, of which 3 were waited for; matrix products, arithmetic and copies ran while one was open for 0% of the time, Pallas kernels for 3%

profile of v6, /device:TPU:1, one launch (start us, length us, event | category | flops | bytes accessed | tf_op | source)
XLA Modules:
  0.0 56.4 jit_solution(14629188613206129061)
XLA Ops:
  0.0 0.0 copy-start.2
  0.0 0.0 copy-start.1
  0.0 1.9 %select.1 = (f32[512,512]{1,0:T(8,128)S(1)}, f32[8,128]{1,0:T(8,128)S(1)}, s32[16,8,128]{2,1,0:T(8,128)S(1)}) custom-call(s32[1,16]{1,0:T(1,128)} %occ_ref.1, s32[1,16]{1,0:T(1,128)} %offset_ref.1, s32[1,16]{1,0:T(1,128)} %other_ref.1, s32[1,16]{1,0:T(1,128)} %blocks_ref.1, f32[4,128,1024]{2,1,0:T(8,128)} %coef_ref.3), custom_call_target="tpu_custom_call" | custom-call | bytes 3145728 | tf_op jit(solution)/shard_map/select/pallas_call | solution.py:169
  1.9 8.1 %collective-permute-start.4 = (f32[512,512]{1,0:T(8,128)S(1)}, f32[512,512]{1,0:T(8,128)S(1)}, u32[]{:S(2)}, u32[]{:S(2)}) collective-permute-start(f32[512,512]{1,0:T(8,128)S(1)} %get-tuple-element.18.own_ref), channel_id=1, source_target_pairs={{0,16},{1,497},{2,18},{3,499},{4,20},{5,501},{6,22},{7,503},{8,24}... | collective-permute-start | bytes 3145736 | tf_op jit(solution)/shard_map/ppermute | solution.py:192
  10.0 1.9 %collective-permute-start.3 = (f32[512,512]{1,0:T(8,128)S(1)}, f32[512,512]{1,0:T(8,128)S(1)}, u32[]{:S(2)}, u32[]{:S(2)}) collective-permute-start(f32[512,512]{1,0:T(8,128)S(1)} %get-tuple-element.18.own_ref), channel_id=1, source_target_pairs={{0,496},{1,17},{2,498},{3,19},{4,500},{5,21},{6,502},{7,23},{8,504... | collective-permute-start | bytes 3145736 | tf_op jit(solution)/shard_map/ppermute | solution.py:192
  11.9 0.0 copy-done.2
  11.9 0.0 copy-done.1
  12.0 1.3 %lagrangian.1 = (f32[776,128]{1,0:T(8,128)S(1)}, f32[776,128]{1,0:T(8,128)S(1)}, f32[520,128]{1,0:T(8,128)S(1)}) custom-call(f32[8,128]{1,0:T(8,128)S(1)} %get-tuple-element.13.meta_ref, s32[16,8,128]{2,1,0:T(8,128)S(1)} %get-tuple-element.14.kept_ref, f32[1,16,128,128]{3,2,1,0:T(8,128)S(1)} %copy-done.1, f32[1,16,128,128]{3,2,1,0:T(8,128)S(1)} %copy-done.2), custom_call_target="tpu_custom_call" | custom-call | flops 201326592 | bytes 3145728 | tf_op jit(solution)/shard_map/lagrangian/pallas_call | solution.py:197
  13.3 4.0 %collective-permute-start = (f32[776,128]{1,0:T(8,128)S(1)}, f32[776,128]{1,0:T(8,128)S(1)}, u32[]{:S(2)}, u32[]{:S(2)}) collective-permute-start(f32[776,128]{1,0:T(8,128)S(1)} %get-tuple-element.16), channel_id=1, source_target_pairs={{0,2},{1,3},{2,4},{3,5},{4,6},{5,7},{6,8},{7,9},{8,10},{9,11},{10,... | collective-permute-start | bytes 1191944 | tf_op jit(solution)/shard_map/ppermute | solution.py:206
  17.3 8.6 %collective-permute-start.1 = (f32[520,128]{1,0:T(8,128)S(1)}, f32[520,128]{1,0:T(8,128)S(1)}, u32[]{:S(2)}, u32[]{:S(2)}) collective-permute-start(f32[520,128]{1,0:T(8,128)S(1)} %get-tuple-element.17), channel_id=1, source_target_pairs={{0,14},{1,15},{2,0},{3,1},{4,2},{5,3},{6,4},{7,5},{8,6},{9,7},{10,... | collective-permute-start | bytes 798728 | tf_op jit(solution)/shard_map/ppermute | solution.py:206
  25.9 3.9 %collective-permute-done.1.above_ref = f32[520,128]{1,0:T(8,128)S(1)} collective-permute-done((f32[520,128]{1,0:T(8,128)S(1)}, f32[520,128]{1,0:T(8,128)S(1)}, u32[]{:S(2)}, u32[]{:S(2)}) %collective-permute-start.1) | collective-permute-done | bytes 266272 | tf_op jit(solution)/shard_map/ppermute | solution.py:206
  29.8 1.9 %collective-permute-done.below_ref = f32[776,128]{1,0:T(8,128)S(1)} collective-permute-done((f32[776,128]{1,0:T(8,128)S(1)}, f32[776,128]{1,0:T(8,128)S(1)}, u32[]{:S(2)}, u32[]{:S(2)}) %collective-permute-start) | collective-permute-done | bytes 397344 | tf_op jit(solution)/shard_map/ppermute | solution.py:206
  31.7 0.4 gather.1.mine_ref
  32.1 4.3 %collective-permute-start.2 = (f32[48,48,128]{2,1,0:T(8,128)S(1)}, f32[48,48,128]{2,1,0:T(8,128)S(1)}, u32[]{:S(2)}, u32[]{:S(2)}) collective-permute-start(f32[48,48,128]{2,1,0:T(8,128)S(1)} %gather.1.mine_ref), channel_id=1, source_target_pairs={{0,1},{1,0},{2,3},{3,2},{4,5},{5,4},{6,7},{7,6},{8,9},{9,8},{10,11... | collective-permute-start | bytes 3538952 | tf_op jit(solution)/shard_map/ppermute | solution.py:214
  36.4 0.0 collective-permute-done.4.first_ref
  36.4 0.0 collective-permute-done.3.second_ref
  36.4 2.4 %collective-permute-done.2.other_ref = f32[48,48,128]{2,1,0:T(8,128)S(1)} collective-permute-done((f32[48,48,128]{2,1,0:T(8,128)S(1)}, f32[48,48,128]{2,1,0:T(8,128)S(1)}, u32[]{:S(2)}, u32[]{:S(2)}) %collective-permute-start.2) | collective-permute-done | bytes 1179680 | tf_op jit(solution)/shard_map/ppermute | solution.py:214
  38.8 0.0 copy-start
  38.8 1.2 %images.1 = f32[8,96,128]{2,1,0:T(8,128)S(1)} custom-call(f32[48,48,128]{2,1,0:T(8,128)S(1)} %gather.1.mine_ref, f32[48,48,128]{2,1,0:T(8,128)S(1)} %collective-permute-done.2.other_ref, f32[512,512]{1,0:T(8,128)S(1)} %get-tuple-element.19.second_ref, f32[512,512]{1,0:T(8,128)S(1)} %get-tuple-element.18.own_ref, f32[512,512]{1,0:T(8,128)S(1)} %get-tuple-element.20.first_ref), custom_call_target="tpu_custom_call" | custom-call | flops 905969664 | bytes 4194304 | tf_op jit(solution)/shard_map/images/pallas_call | solution.py:227
  40.1 15.1 %all_to_all.5.part_ref = f32[8,96,128]{2,1,0:T(8,128)S(1)} all-to-all(f32[8,96,128]{2,1,0:T(8,128)S(1)} %images.1), channel_id=1, replica_groups={{12,14,8,10,6,4,2,0},{13,15,9,11,7,5,3,1},{28,30,24,26,22,20,18,16},{29..., dimensions={0} | all-to-all | bytes 786432 | tf_op jit(solution)/shard_map/all_to_all | solution.py:235
  55.2 0.0 copy-done
  55.2 1.2 %density.1 = f32[64,1024]{1,0:T(8,128)} custom-call(f32[8,96,128]{2,1,0:T(8,128)S(1)} %all_to_all.5.part_ref, f32[4,128,1024]{2,1,0:T(8,128)S(1)} %copy-done), custom_call_target="tpu_custom_call" | custom-call | flops 201326592 | bytes 3145728 | tf_op jit(solution)/shard_map/density/pallas_call | solution.py:237
  (1 shorter events, 0.0 us)
Async XLA Ops:
  0.0 11.9 %copy-start.2 = (f32[1,16,128,128]{3,2,1,0:T(8,128)S(1)}, f32[1,16,128,128]{3,2,1,0:T(8,128)}, u32[]{:S(2)}) copy-start(f32[1,16,128,128]{3,2,1,0:T(8,128)} %int_ref.1) | copy-start | bytes 3145732
  0.0 11.9 %copy-start.1 = (f32[1,16,128,128]{3,2,1,0:T(8,128)S(1)}, f32[1,16,128,128]{3,2,1,0:T(8,128)}, u32[]{:S(2)}) copy-start(f32[1,16,128,128]{3,2,1,0:T(8,128)} %amp_ref.1) | copy-start | bytes 3145732
  1.9 34.5 %collective-permute-start.4 = (f32[512,512]{1,0:T(8,128)S(1)}, f32[512,512]{1,0:T(8,128)S(1)}, u32[]{:S(2)}, u32[]{:S(2)}) collective-permute-start(f32[512,512]{1,0:T(8,128)S(1)} %get-tuple-element.18.own_ref), channel_id=1, source_target_pairs={{0,16},{1,497},{2,18},{3,499},{4,20},{5,501},{6,22},{7,503},{8,24}... | collective-permute-start | bytes 3145736 | tf_op jit(solution)/shard_map/ppermute | solution.py:192
  10.0 26.4 %collective-permute-start.3 = (f32[512,512]{1,0:T(8,128)S(1)}, f32[512,512]{1,0:T(8,128)S(1)}, u32[]{:S(2)}, u32[]{:S(2)}) collective-permute-start(f32[512,512]{1,0:T(8,128)S(1)} %get-tuple-element.18.own_ref), channel_id=1, source_target_pairs={{0,496},{1,17},{2,498},{3,19},{4,500},{5,21},{6,502},{7,23},{8,504... | collective-permute-start | bytes 3145736 | tf_op jit(solution)/shard_map/ppermute | solution.py:192
  13.3 18.4 %collective-permute-start = (f32[776,128]{1,0:T(8,128)S(1)}, f32[776,128]{1,0:T(8,128)S(1)}, u32[]{:S(2)}, u32[]{:S(2)}) collective-permute-start(f32[776,128]{1,0:T(8,128)S(1)} %get-tuple-element.16), channel_id=1, source_target_pairs={{0,2},{1,3},{2,4},{3,5},{4,6},{5,7},{6,8},{7,9},{8,10},{9,11},{10,... | collective-permute-start | bytes 1191944 | tf_op jit(solution)/shard_map/ppermute | solution.py:206
  17.3 12.5 %collective-permute-start.1 = (f32[520,128]{1,0:T(8,128)S(1)}, f32[520,128]{1,0:T(8,128)S(1)}, u32[]{:S(2)}, u32[]{:S(2)}) collective-permute-start(f32[520,128]{1,0:T(8,128)S(1)} %get-tuple-element.17), channel_id=1, source_target_pairs={{0,14},{1,15},{2,0},{3,1},{4,2},{5,3},{6,4},{7,5},{8,6},{9,7},{10,... | collective-permute-start | bytes 798728 | tf_op jit(solution)/shard_map/ppermute | solution.py:206
  32.1 6.8 %collective-permute-start.2 = (f32[48,48,128]{2,1,0:T(8,128)S(1)}, f32[48,48,128]{2,1,0:T(8,128)S(1)}, u32[]{:S(2)}, u32[]{:S(2)}) collective-permute-start(f32[48,48,128]{2,1,0:T(8,128)S(1)} %gather.1.mine_ref), channel_id=1, source_target_pairs={{0,1},{1,0},{2,3},{3,2},{4,5},{5,4},{6,7},{7,6},{8,9},{9,8},{10,11... | collective-permute-start | bytes 3538952 | tf_op jit(solution)/shard_map/ppermute | solution.py:214
  38.8 16.4 %copy-start = (f32[4,128,1024]{2,1,0:T(8,128)S(1)}, f32[4,128,1024]{2,1,0:T(8,128)}, u32[]{:S(2)}) copy-start(f32[4,128,1024]{2,1,0:T(8,128)} %coef_ref.3) | copy-start | bytes 6291460

commit v7 on v6

--- a/solution.py
+++ b/solution.py
@@ -15,7 +15,7 @@
 SLOTS = 16
 CHIPS = 8
 WIDE = AO // 2
-ORDER = (6, 7, 4, 5, 3, 2, 1, 0)
+ORDER = (7, 4, 6, 5, 3, 2, 1, 0)
 NARROW = AO // 16
 PART = 16
 HELD = 3 * PART

time: 56.7 us -> 56.3 us (level)
  no operation moved by 1% of the time
where the time goes in v7:
time: 56.3 us; the launch traced here: 56 us
  starting transfers between devices  27 us (48%)
  blocking collectives  14.7 us (26%)
  waiting for transfers between devices  8.24 us (15%)
  Pallas kernels  5.96 us (11%)
    all_to_all x1, blocking collectives, local(): parts = lax.all_to_all(parts, 'col', 0, 0, axis_index_groups=groups)  14.7 us
    ppermute x2, starting transfers between devices, local(): lax.ppermute(x, 'col', [(i, (i + 2 * chips) % devices) for i in range(dev...  12.6 us
    ppermute x2, starting transfers between devices, halo(): return lax.ppermute(own, ('blk', 'col'), pairs)  10 us
    ppermute x2, waiting for transfers between devices, local(): lax.ppermute(x, 'col', [(i, (i + 2 * chips) % devices) for i in range(dev...  5.81 us
    ppermute x1, starting transfers between devices, local(): other = lax.ppermute(mine, 'col', [(i, i ^ 1) for i in range(devices)])  4.31 us
    ppermute x1, waiting for transfers between devices, local(): other = lax.ppermute(mine, 'col', [(i, i ^ 1) for i in range(devices)])  2.42 us
    pallas_call x1, Pallas kernels, local(): pl.pallas_call(select_kernel, in_specs=[pl.BlockSpec(memory_space=pltpu.H...  1.87 us
    pallas_call x1, Pallas kernels, local(): pl.pallas_call(lagrangian_kernel, out_shape=(pieces(HELD), pieces(HELD),...  1.29 us
  transfers between devices with their start and end apart: 5, of which 3 were waited for; matrix products, arithmetic and copies ran while one was open for 0% of the time, Pallas kernels for 3%

profile of v7, /device:TPU:1, one launch (start us, length us, event | category | flops | bytes accessed | tf_op | source)
XLA Modules:
  0.0 56.0 jit_solution(5696211728278216017)
XLA Ops:
  0.0 0.0 copy-start.2
  0.0 0.0 copy-start.1
  0.0 1.9 %select.1 = (f32[512,512]{1,0:T(8,128)S(1)}, f32[8,128]{1,0:T(8,128)S(1)}, s32[16,8,128]{2,1,0:T(8,128)S(1)}) custom-call(s32[1,16]{1,0:T(1,128)} %occ_ref.1, s32[1,16]{1,0:T(1,128)} %offset_ref.1, s32[1,16]{1,0:T(1,128)} %other_ref.1, s32[1,16]{1,0:T(1,128)} %blocks_ref.1, f32[4,128,1024]{2,1,0:T(8,128)} %coef_ref.3), custom_call_target="tpu_custom_call" | custom-call | bytes 3145728 | tf_op jit(solution)/shard_map/select/pallas_call | solution.py:169
  1.9 8.1 %collective-permute-start.4 = (f32[512,512]{1,0:T(8,128)S(1)}, f32[512,512]{1,0:T(8,128)S(1)}, u32[]{:S(2)}, u32[]{:S(2)}) collective-permute-start(f32[512,512]{1,0:T(8,128)S(1)} %get-tuple-element.18.own_ref), channel_id=1, source_target_pairs={{0,16},{1,497},{2,18},{3,499},{4,20},{5,501},{6,22},{7,503},{8,24}... | collective-permute-start | bytes 3145736 | tf_op jit(solution)/shard_map/ppermute | solution.py:192
  10.0 1.9 %collective-permute-start.3 = (f32[512,512]{1,0:T(8,128)S(1)}, f32[512,512]{1,0:T(8,128)S(1)}, u32[]{:S(2)}, u32[]{:S(2)}) collective-permute-start(f32[512,512]{1,0:T(8,128)S(1)} %get-tuple-element.18.own_ref), channel_id=1, source_target_pairs={{0,496},{1,17},{2,498},{3,19},{4,500},{5,21},{6,502},{7,23},{8,504... | collective-permute-start | bytes 3145736 | tf_op jit(solution)/shard_map/ppermute | solution.py:192
  11.9 0.0 copy-done.2
  11.9 0.0 copy-done.1
  12.0 1.3 %lagrangian.1 = (f32[776,128]{1,0:T(8,128)S(1)}, f32[776,128]{1,0:T(8,128)S(1)}, f32[520,128]{1,0:T(8,128)S(1)}) custom-call(f32[8,128]{1,0:T(8,128)S(1)} %get-tuple-element.13.meta_ref, s32[16,8,128]{2,1,0:T(8,128)S(1)} %get-tuple-element.14.kept_ref, f32[1,16,128,128]{3,2,1,0:T(8,128)S(1)} %copy-done.1, f32[1,16,128,128]{3,2,1,0:T(8,128)S(1)} %copy-done.2), custom_call_target="tpu_custom_call" | custom-call | flops 201326592 | bytes 3145728 | tf_op jit(solution)/shard_map/lagrangian/pallas_call | solution.py:197
  13.3 4.0 %collective-permute-start = (f32[776,128]{1,0:T(8,128)S(1)}, f32[776,128]{1,0:T(8,128)S(1)}, u32[]{:S(2)}, u32[]{:S(2)}) collective-permute-start(f32[776,128]{1,0:T(8,128)S(1)} %get-tuple-element.16), channel_id=1, source_target_pairs={{0,2},{1,3},{2,4},{3,5},{4,6},{5,7},{6,8},{7,9},{8,10},{9,11},{10,... | collective-permute-start | bytes 1191944 | tf_op jit(solution)/shard_map/ppermute | solution.py:206
  17.3 8.6 %collective-permute-start.1 = (f32[520,128]{1,0:T(8,128)S(1)}, f32[520,128]{1,0:T(8,128)S(1)}, u32[]{:S(2)}, u32[]{:S(2)}) collective-permute-start(f32[520,128]{1,0:T(8,128)S(1)} %get-tuple-element.17), channel_id=1, source_target_pairs={{0,14},{1,15},{2,0},{3,1},{4,2},{5,3},{6,4},{7,5},{8,6},{9,7},{10,... | collective-permute-start | bytes 798728 | tf_op jit(solution)/shard_map/ppermute | solution.py:206
  25.9 3.9 %collective-permute-done.1.above_ref = f32[520,128]{1,0:T(8,128)S(1)} collective-permute-done((f32[520,128]{1,0:T(8,128)S(1)}, f32[520,128]{1,0:T(8,128)S(1)}, u32[]{:S(2)}, u32[]{:S(2)}) %collective-permute-start.1) | collective-permute-done | bytes 266272 | tf_op jit(solution)/shard_map/ppermute | solution.py:206
  29.8 1.9 %collective-permute-done.below_ref = f32[776,128]{1,0:T(8,128)S(1)} collective-permute-done((f32[776,128]{1,0:T(8,128)S(1)}, f32[776,128]{1,0:T(8,128)S(1)}, u32[]{:S(2)}, u32[]{:S(2)}) %collective-permute-start) | collective-permute-done | bytes 397344 | tf_op jit(solution)/shard_map/ppermute | solution.py:206
  31.7 0.4 gather.1.mine_ref
  32.1 4.3 %collective-permute-start.2 = (f32[48,48,128]{2,1,0:T(8,128)S(1)}, f32[48,48,128]{2,1,0:T(8,128)S(1)}, u32[]{:S(2)}, u32[]{:S(2)}) collective-permute-start(f32[48,48,128]{2,1,0:T(8,128)S(1)} %gather.1.mine_ref), channel_id=1, source_target_pairs={{0,1},{1,0},{2,3},{3,2},{4,5},{5,4},{6,7},{7,6},{8,9},{9,8},{10,11... | collective-permute-start | bytes 3538952 | tf_op jit(solution)/shard_map/ppermute | solution.py:214
  36.4 0.0 collective-permute-done.4.first_ref
  36.4 0.0 collective-permute-done.3.second_ref
  36.4 2.4 %collective-permute-done.2.other_ref = f32[48,48,128]{2,1,0:T(8,128)S(1)} collective-permute-done((f32[48,48,128]{2,1,0:T(8,128)S(1)}, f32[48,48,128]{2,1,0:T(8,128)S(1)}, u32[]{:S(2)}, u32[]{:S(2)}) %collective-permute-start.2) | collective-permute-done | bytes 1179680 | tf_op jit(solution)/shard_map/ppermute | solution.py:214
  38.8 0.0 copy-start
  38.8 1.2 %images.1 = f32[8,96,128]{2,1,0:T(8,128)S(1)} custom-call(f32[48,48,128]{2,1,0:T(8,128)S(1)} %gather.1.mine_ref, f32[48,48,128]{2,1,0:T(8,128)S(1)} %collective-permute-done.2.other_ref, f32[512,512]{1,0:T(8,128)S(1)} %get-tuple-element.19.second_ref, f32[512,512]{1,0:T(8,128)S(1)} %get-tuple-element.18.own_ref, f32[512,512]{1,0:T(8,128)S(1)} %get-tuple-element.20.first_ref), custom_call_target="tpu_custom_call" | custom-call | flops 905969664 | bytes 4194304 | tf_op jit(solution)/shard_map/images/pallas_call | solution.py:227
  40.1 14.7 %all_to_all.5.part_ref = f32[8,96,128]{2,1,0:T(8,128)S(1)} all-to-all(f32[8,96,128]{2,1,0:T(8,128)S(1)} %images.1), channel_id=1, replica_groups={{14,8,12,10,6,4,2,0},{15,9,13,11,7,5,3,1},{30,24,28,26,22,20,18,16},{31..., dimensions={0} | all-to-all | bytes 786432 | tf_op jit(solution)/shard_map/all_to_all | solution.py:235
  54.8 0.0 copy-done
  54.8 1.2 %density.1 = f32[64,1024]{1,0:T(8,128)} custom-call(f32[8,96,128]{2,1,0:T(8,128)S(1)} %all_to_all.5.part_ref, f32[4,128,1024]{2,1,0:T(8,128)S(1)} %copy-done), custom_call_target="tpu_custom_call" | custom-call | flops 201326592 | bytes 3145728 | tf_op jit(solution)/shard_map/density/pallas_call | solution.py:237
  (1 shorter events, 0.0 us)
Async XLA Ops:
  0.0 11.9 %copy-start.2 = (f32[1,16,128,128]{3,2,1,0:T(8,128)S(1)}, f32[1,16,128,128]{3,2,1,0:T(8,128)}, u32[]{:S(2)}) copy-start(f32[1,16,128,128]{3,2,1,0:T(8,128)} %int_ref.1) | copy-start | bytes 3145732
  0.0 11.9 %copy-start.1 = (f32[1,16,128,128]{3,2,1,0:T(8,128)S(1)}, f32[1,16,128,128]{3,2,1,0:T(8,128)}, u32[]{:S(2)}) copy-start(f32[1,16,128,128]{3,2,1,0:T(8,128)} %amp_ref.1) | copy-start | bytes 3145732
  1.9 34.5 %collective-permute-start.4 = (f32[512,512]{1,0:T(8,128)S(1)}, f32[512,512]{1,0:T(8,128)S(1)}, u32[]{:S(2)}, u32[]{:S(2)}) collective-permute-start(f32[512,512]{1,0:T(8,128)S(1)} %get-tuple-element.18.own_ref), channel_id=1, source_target_pairs={{0,16},{1,497},{2,18},{3,499},{4,20},{5,501},{6,22},{7,503},{8,24}... | collective-permute-start | bytes 3145736 | tf_op jit(solution)/shard_map/ppermute | solution.py:192
  10.0 26.4 %collective-permute-start.3 = (f32[512,512]{1,0:T(8,128)S(1)}, f32[512,512]{1,0:T(8,128)S(1)}, u32[]{:S(2)}, u32[]{:S(2)}) collective-permute-start(f32[512,512]{1,0:T(8,128)S(1)} %get-tuple-element.18.own_ref), channel_id=1, source_target_pairs={{0,496},{1,17},{2,498},{3,19},{4,500},{5,21},{6,502},{7,23},{8,504... | collective-permute-start | bytes 3145736 | tf_op jit(solution)/shard_map/ppermute | solution.py:192
  13.3 18.4 %collective-permute-start = (f32[776,128]{1,0:T(8,128)S(1)}, f32[776,128]{1,0:T(8,128)S(1)}, u32[]{:S(2)}, u32[]{:S(2)}) collective-permute-start(f32[776,128]{1,0:T(8,128)S(1)} %get-tuple-element.16), channel_id=1, source_target_pairs={{0,2},{1,3},{2,4},{3,5},{4,6},{5,7},{6,8},{7,9},{8,10},{9,11},{10,... | collective-permute-start | bytes 1191944 | tf_op jit(solution)/shard_map/ppermute | solution.py:206
  17.3 12.5 %collective-permute-start.1 = (f32[520,128]{1,0:T(8,128)S(1)}, f32[520,128]{1,0:T(8,128)S(1)}, u32[]{:S(2)}, u32[]{:S(2)}) collective-permute-start(f32[520,128]{1,0:T(8,128)S(1)} %get-tuple-element.17), channel_id=1, source_target_pairs={{0,14},{1,15},{2,0},{3,1},{4,2},{5,3},{6,4},{7,5},{8,6},{9,7},{10,... | collective-permute-start | bytes 798728 | tf_op jit(solution)/shard_map/ppermute | solution.py:206
  32.1 6.8 %collective-permute-start.2 = (f32[48,48,128]{2,1,0:T(8,128)S(1)}, f32[48,48,128]{2,1,0:T(8,128)S(1)}, u32[]{:S(2)}, u32[]{:S(2)}) collective-permute-start(f32[48,48,128]{2,1,0:T(8,128)S(1)} %gather.1.mine_ref), channel_id=1, source_target_pairs={{0,1},{1,0},{2,3},{3,2},{4,5},{5,4},{6,7},{7,6},{8,9},{9,8},{10,11... | collective-permute-start | bytes 3538952 | tf_op jit(solution)/shard_map/ppermute | solution.py:214
  38.8 16.0 %copy-start = (f32[4,128,1024]{2,1,0:T(8,128)S(1)}, f32[4,128,1024]{2,1,0:T(8,128)}, u32[]{:S(2)}) copy-start(f32[4,128,1024]{2,1,0:T(8,128)} %coef_ref.3) | copy-start | bytes 6291460

commit v8 on v7

--- a/solution.py
+++ b/solution.py
@@ -137,8 +137,8 @@
     sums = jnp.concatenate(sums, axis=0).T
     lhs = jnp.concatenate(split(jnp.concatenate([sums[:NARROW], sums[NARROW:]], axis=1)))
     copies = []
-    for n in range(4):
-        at = slice(256 * n, 256 * (n + 1))
+    for n in range(2):
+        at = slice(512 * n, 512 * (n + 1))
         rhs = [
             coef_ref[2 * pair + o, r * PART : (r + 1) * PART, at]
             for pair in range(2)
@@ -238,7 +238,7 @@
         density_kernel,
         out_specs=pl.BlockSpec(memory_space=pl.ANY),
         out_shape=jax.ShapeDtypeStruct((NARROW, AO), F32),
-        scratch_shapes=[pltpu.VMEM((NARROW, AO), F32), pltpu.SemaphoreType.DMA((4,))],
+        scratch_shapes=[pltpu.VMEM((NARROW, AO), F32), pltpu.SemaphoreType.DMA((2,))],
         compiler_params=PARAMS,
         cost_estimate=cost(3 * ORB * PNO * NARROW * AO, 3 << 20),
         name="density",

time: 56.3 us -> 56.3 us (level)
  no operation moved by 1% of the time
where the time goes in v8:
time: 56.3 us; the launch traced here: 56 us
  starting transfers between devices  27 us (48%)
  blocking collectives  14.7 us (26%)
  waiting for transfers between devices  8.24 us (15%)
  Pallas kernels  5.95 us (11%)
    all_to_all x1, blocking collectives, local(): parts = lax.all_to_all(parts, 'col', 0, 0, axis_index_groups=groups)  14.7 us
    ppermute x2, starting transfers between devices, local(): lax.ppermute(x, 'col', [(i, (i + 2 * chips) % devices) for i in range(dev...  12.6 us
    ppermute x2, starting transfers between devices, halo(): return lax.ppermute(own, ('blk', 'col'), pairs)  10 us
    ppermute x2, waiting for transfers between devices, local(): lax.ppermute(x, 'col', [(i, (i + 2 * chips) % devices) for i in range(dev...  5.81 us
    ppermute x1, starting transfers between devices, local(): other = lax.ppermute(mine, 'col', [(i, i ^ 1) for i in range(devices)])  4.31 us
    ppermute x1, waiting for transfers between devices, local(): other = lax.ppermute(mine, 'col', [(i, i ^ 1) for i in range(devices)])  2.42 us
    pallas_call x1, Pallas kernels, local(): pl.pallas_call(select_kernel, in_specs=[pl.BlockSpec(memory_space=pltpu.H...  1.87 us
    pallas_call x1, Pallas kernels, local(): pl.pallas_call(lagrangian_kernel, out_shape=(pieces(HELD), pieces(HELD),...  1.29 us
  transfers between devices with their start and end apart: 5, of which 3 were waited for; matrix products, arithmetic and copies ran while one was open for 0% of the time, Pallas kernels for 3%

profile of v8, /device:TPU:1, one launch (start us, length us, event | category | flops | bytes accessed | tf_op | source)
XLA Modules:
  0.0 56.0 jit_solution(5752154440115324141)
XLA Ops:
  0.0 0.0 copy-start.2
  0.0 0.0 copy-start.1
  0.0 1.9 %select.1 = (f32[512,512]{1,0:T(8,128)S(1)}, f32[8,128]{1,0:T(8,128)S(1)}, s32[16,8,128]{2,1,0:T(8,128)S(1)}) custom-call(s32[1,16]{1,0:T(1,128)} %occ_ref.1, s32[1,16]{1,0:T(1,128)} %offset_ref.1, s32[1,16]{1,0:T(1,128)} %other_ref.1, s32[1,16]{1,0:T(1,128)} %blocks_ref.1, f32[4,128,1024]{2,1,0:T(8,128)} %coef_ref.3), custom_call_target="tpu_custom_call" | custom-call | bytes 3145728 | tf_op jit(solution)/shard_map/select/pallas_call | solution.py:169
  1.9 8.1 %collective-permute-start.4 = (f32[512,512]{1,0:T(8,128)S(1)}, f32[512,512]{1,0:T(8,128)S(1)}, u32[]{:S(2)}, u32[]{:S(2)}) collective-permute-start(f32[512,512]{1,0:T(8,128)S(1)} %get-tuple-element.18.own_ref), channel_id=1, source_target_pairs={{0,16},{1,497},{2,18},{3,499},{4,20},{5,501},{6,22},{7,503},{8,24}... | collective-permute-start | bytes 3145736 | tf_op jit(solution)/shard_map/ppermute | solution.py:192
  10.0 1.9 %collective-permute-start.3 = (f32[512,512]{1,0:T(8,128)S(1)}, f32[512,512]{1,0:T(8,128)S(1)}, u32[]{:S(2)}, u32[]{:S(2)}) collective-permute-start(f32[512,512]{1,0:T(8,128)S(1)} %get-tuple-element.18.own_ref), channel_id=1, source_target_pairs={{0,496},{1,17},{2,498},{3,19},{4,500},{5,21},{6,502},{7,23},{8,504... | collective-permute-start | bytes 3145736 | tf_op jit(solution)/shard_map/ppermute | solution.py:192
  11.9 0.0 copy-done.2
  11.9 0.0 copy-done.1
  12.0 1.3 %lagrangian.1 = (f32[776,128]{1,0:T(8,128)S(1)}, f32[776,128]{1,0:T(8,128)S(1)}, f32[520,128]{1,0:T(8,128)S(1)}) custom-call(f32[8,128]{1,0:T(8,128)S(1)} %get-tuple-element.13.meta_ref, s32[16,8,128]{2,1,0:T(8,128)S(1)} %get-tuple-element.14.kept_ref, f32[1,16,128,128]{3,2,1,0:T(8,128)S(1)} %copy-done.1, f32[1,16,128,128]{3,2,1,0:T(8,128)S(1)} %copy-done.2), custom_call_target="tpu_custom_call" | custom-call | flops 201326592 | bytes 3145728 | tf_op jit(solution)/shard_map/lagrangian/pallas_call | solution.py:197
  13.3 4.0 %collective-permute-start = (f32[776,128]{1,0:T(8,128)S(1)}, f32[776,128]{1,0:T(8,128)S(1)}, u32[]{:S(2)}, u32[]{:S(2)}) collective-permute-start(f32[776,128]{1,0:T(8,128)S(1)} %get-tuple-element.16), channel_id=1, source_target_pairs={{0,2},{1,3},{2,4},{3,5},{4,6},{5,7},{6,8},{7,9},{8,10},{9,11},{10,... | collective-permute-start | bytes 1191944 | tf_op jit(solution)/shard_map/ppermute | solution.py:206
  17.3 8.6 %collective-permute-start.1 = (f32[520,128]{1,0:T(8,128)S(1)}, f32[520,128]{1,0:T(8,128)S(1)}, u32[]{:S(2)}, u32[]{:S(2)}) collective-permute-start(f32[520,128]{1,0:T(8,128)S(1)} %get-tuple-element.17), channel_id=1, source_target_pairs={{0,14},{1,15},{2,0},{3,1},{4,2},{5,3},{6,4},{7,5},{8,6},{9,7},{10,... | collective-permute-start | bytes 798728 | tf_op jit(solution)/shard_map/ppermute | solution.py:206
  25.9 3.9 %collective-permute-done.1.above_ref = f32[520,128]{1,0:T(8,128)S(1)} collective-permute-done((f32[520,128]{1,0:T(8,128)S(1)}, f32[520,128]{1,0:T(8,128)S(1)}, u32[]{:S(2)}, u32[]{:S(2)}) %collective-permute-start.1) | collective-permute-done | bytes 266272 | tf_op jit(solution)/shard_map/ppermute | solution.py:206
  29.8 1.9 %collective-permute-done.below_ref = f32[776,128]{1,0:T(8,128)S(1)} collective-permute-done((f32[776,128]{1,0:T(8,128)S(1)}, f32[776,128]{1,0:T(8,128)S(1)}, u32[]{:S(2)}, u32[]{:S(2)}) %collective-permute-start) | collective-permute-done | bytes 397344 | tf_op jit(solution)/shard_map/ppermute | solution.py:206
  31.7 0.4 gather.1.mine_ref
  32.1 4.3 %collective-permute-start.2 = (f32[48,48,128]{2,1,0:T(8,128)S(1)}, f32[48,48,128]{2,1,0:T(8,128)S(1)}, u32[]{:S(2)}, u32[]{:S(2)}) collective-permute-start(f32[48,48,128]{2,1,0:T(8,128)S(1)} %gather.1.mine_ref), channel_id=1, source_target_pairs={{0,1},{1,0},{2,3},{3,2},{4,5},{5,4},{6,7},{7,6},{8,9},{9,8},{10,11... | collective-permute-start | bytes 3538952 | tf_op jit(solution)/shard_map/ppermute | solution.py:214
  36.4 0.0 collective-permute-done.4.first_ref
  36.4 0.0 collective-permute-done.3.second_ref
  36.4 2.4 %collective-permute-done.2.other_ref = f32[48,48,128]{2,1,0:T(8,128)S(1)} collective-permute-done((f32[48,48,128]{2,1,0:T(8,128)S(1)}, f32[48,48,128]{2,1,0:T(8,128)S(1)}, u32[]{:S(2)}, u32[]{:S(2)}) %collective-permute-start.2) | collective-permute-done | bytes 1179680 | tf_op jit(solution)/shard_map/ppermute | solution.py:214
  38.8 0.0 copy-start
  38.8 1.2 %images.1 = f32[8,96,128]{2,1,0:T(8,128)S(1)} custom-call(f32[48,48,128]{2,1,0:T(8,128)S(1)} %gather.1.mine_ref, f32[48,48,128]{2,1,0:T(8,128)S(1)} %collective-permute-done.2.other_ref, f32[512,512]{1,0:T(8,128)S(1)} %get-tuple-element.19.second_ref, f32[512,512]{1,0:T(8,128)S(1)} %get-tuple-element.18.own_ref, f32[512,512]{1,0:T(8,128)S(1)} %get-tuple-element.20.first_ref), custom_call_target="tpu_custom_call" | custom-call | flops 905969664 | bytes 4194304 | tf_op jit(solution)/shard_map/images/pallas_call | solution.py:227
  40.1 14.7 %all_to_all.5.part_ref = f32[8,96,128]{2,1,0:T(8,128)S(1)} all-to-all(f32[8,96,128]{2,1,0:T(8,128)S(1)} %images.1), channel_id=1, replica_groups={{14,8,12,10,6,4,2,0},{15,9,13,11,7,5,3,1},{30,24,28,26,22,20,18,16},{31..., dimensions={0} | all-to-all | bytes 786432 | tf_op jit(solution)/shard_map/all_to_all | solution.py:235
  54.8 0.0 copy-done
  54.8 1.2 %density.1 = f32[64,1024]{1,0:T(8,128)} custom-call(f32[8,96,128]{2,1,0:T(8,128)S(1)} %all_to_all.5.part_ref, f32[4,128,1024]{2,1,0:T(8,128)S(1)} %copy-done), custom_call_target="tpu_custom_call" | custom-call | flops 201326592 | bytes 3145728 | tf_op jit(solution)/shard_map/density/pallas_call | solution.py:237
  (1 shorter events, 0.0 us)
Async XLA Ops:
  0.0 11.9 %copy-start.2 = (f32[1,16,128,128]{3,2,1,0:T(8,128)S(1)}, f32[1,16,128,128]{3,2,1,0:T(8,128)}, u32[]{:S(2)}) copy-start(f32[1,16,128,128]{3,2,1,0:T(8,128)} %int_ref.1) | copy-start | bytes 3145732
  0.0 11.9 %copy-start.1 = (f32[1,16,128,128]{3,2,1,0:T(8,128)S(1)}, f32[1,16,128,128]{3,2,1,0:T(8,128)}, u32[]{:S(2)}) copy-start(f32[1,16,128,128]{3,2,1,0:T(8,128)} %amp_ref.1) | copy-start | bytes 3145732
  1.9 34.5 %collective-permute-start.4 = (f32[512,512]{1,0:T(8,128)S(1)}, f32[512,512]{1,0:T(8,128)S(1)}, u32[]{:S(2)}, u32[]{:S(2)}) collective-permute-start(f32[512,512]{1,0:T(8,128)S(1)} %get-tuple-element.18.own_ref), channel_id=1, source_target_pairs={{0,16},{1,497},{2,18},{3,499},{4,20},{5,501},{6,22},{7,503},{8,24}... | collective-permute-start | bytes 3145736 | tf_op jit(solution)/shard_map/ppermute | solution.py:192
  10.0 26.4 %collective-permute-start.3 = (f32[512,512]{1,0:T(8,128)S(1)}, f32[512,512]{1,0:T(8,128)S(1)}, u32[]{:S(2)}, u32[]{:S(2)}) collective-permute-start(f32[512,512]{1,0:T(8,128)S(1)} %get-tuple-element.18.own_ref), channel_id=1, source_target_pairs={{0,496},{1,17},{2,498},{3,19},{4,500},{5,21},{6,502},{7,23},{8,504... | collective-permute-start | bytes 3145736 | tf_op jit(solution)/shard_map/ppermute | solution.py:192
  13.3 18.4 %collective-permute-start = (f32[776,128]{1,0:T(8,128)S(1)}, f32[776,128]{1,0:T(8,128)S(1)}, u32[]{:S(2)}, u32[]{:S(2)}) collective-permute-start(f32[776,128]{1,0:T(8,128)S(1)} %get-tuple-element.16), channel_id=1, source_target_pairs={{0,2},{1,3},{2,4},{3,5},{4,6},{5,7},{6,8},{7,9},{8,10},{9,11},{10,... | collective-permute-start | bytes 1191944 | tf_op jit(solution)/shard_map/ppermute | solution.py:206
  17.3 12.5 %collective-permute-start.1 = (f32[520,128]{1,0:T(8,128)S(1)}, f32[520,128]{1,0:T(8,128)S(1)}, u32[]{:S(2)}, u32[]{:S(2)}) collective-permute-start(f32[520,128]{1,0:T(8,128)S(1)} %get-tuple-element.17), channel_id=1, source_target_pairs={{0,14},{1,15},{2,0},{3,1},{4,2},{5,3},{6,4},{7,5},{8,6},{9,7},{10,... | collective-permute-start | bytes 798728 | tf_op jit(solution)/shard_map/ppermute | solution.py:206
  32.1 6.8 %collective-permute-start.2 = (f32[48,48,128]{2,1,0:T(8,128)S(1)}, f32[48,48,128]{2,1,0:T(8,128)S(1)}, u32[]{:S(2)}, u32[]{:S(2)}) collective-permute-start(f32[48,48,128]{2,1,0:T(8,128)S(1)} %gather.1.mine_ref), channel_id=1, source_target_pairs={{0,1},{1,0},{2,3},{3,2},{4,5},{5,4},{6,7},{7,6},{8,9},{9,8},{10,11... | collective-permute-start | bytes 3538952 | tf_op jit(solution)/shard_map/ppermute | solution.py:214
  38.8 16.0 %copy-start = (f32[4,128,1024]{2,1,0:T(8,128)S(1)}, f32[4,128,1024]{2,1,0:T(8,128)}, u32[]{:S(2)}) copy-start(f32[4,128,1024]{2,1,0:T(8,128)} %coef_ref.3) | copy-start | bytes 6291460
